TPU v7x, 256 devices: a whole 4x4x8 slice. The times are simulated.
256 devices in a mesh: rows: 32 (over z, y), rhs: 8 (over x, core).
Axes of the slice: x: 4, y: 4, z: 8, core: 2. Of those that a mesh axis runs over, the one named last changes fastest.
Arguments:
- x_t: bfloat16 [64, 131072], P('rhs', 'rows'), may hold values from -6 to 6
- far_v: bfloat16 [32, 64, 64, 512], P('rows', 'rhs'), may hold values from -0.25 to 0.25
- far_u: bfloat16 [32, 64, 64, 4096], P('rows', 'rhs'), may hold values from -0.125 to 0.125
- far_cols: int32 [32, 64], P('rows', 'rhs'), may hold values from 0 to 255, as said below
- rank_class: int32 [32, 64], P('rows', 'rhs'), may hold values from 0 to 2
- near_block: bfloat16 [131072, 4096], P('rows', 'rhs'), may hold values from -0.09375 to 0.09375
Outputs:
- y_t: bfloat16 [64, 131072], P('rhs', 'rows')
Inputs may be any that keep to these rules, and one draw needn't show every extreme that they name: For k * 8 <= b < (k + 1) * 8, far_cols[i, b] * 512 lies in [k * 16384, (k + 1) * 16384) and outside [i * 4096, (i + 1) * 4096); no value repeats within a row cluster.
All inputs are finite; a program needn't handle non-finite values.
Results may differ from a plain program's by a relative error of at most 0.0043.
Values may be sent and summed in bfloat16 or wider, within the bound.
No kernel may reach another device: no remote copies, remote signals or barrier semaphores. Data moves between devices by JAX's collectives and lax.ppermute only.
A program may use at most 128 MiB of HBM per device.

v0:
```python
import jax
import jax.numpy as jnp
from jax import lax
from jax.sharding import PartitionSpec as P


def low_rank(rank_cut, rank_top):

    def low_branch(factor, x_block):
        result = jnp.einsum(
            "rt,ct->rc", factor[:rank_cut], x_block, preferred_element_type=jnp.float32
        ).astype(jnp.bfloat16)
        return jnp.pad(result, ((0, rank_top - rank_cut), (0, 0)))

    return low_branch


def expand(rank_cut):

    def expand_branch(running, factor, coeffs):
        return running + jnp.einsum(
            "rs,rc->cs", factor[:rank_cut], coeffs[:rank_cut], preferred_element_type=jnp.float32
        )

    return expand_branch


def on_device(x_t, far_v, far_u, far_cols, rank_class, near_block):
    rank_top = far_v.shape[2]
    block_width = far_v.shape[3]
    cluster_size = far_u.shape[3]
    levels = (rank_top // 4, rank_top // 2, rank_top)
    project_fns = [low_rank(rank_cut, rank_top) for rank_cut in levels]
    expand_fns = [expand(rank_cut) for rank_cut in levels]
    own_block = lax.all_gather(x_t, "rhs", axis=0, tiled=True)
    source = lax.all_gather(own_block, "rows", axis=1, tiled=True)
    piece_width = near_block.shape[1]
    near_cols = lax.dynamic_slice_in_dim(
        own_block, lax.axis_index("rhs") * piece_width, piece_width, 1
    )
    near_part = jnp.einsum("ct,st->cs", near_cols, near_block, preferred_element_type=jnp.float32)
    column_ids = far_cols[0]
    classes = rank_class[0]
    factors_v = far_v[0]
    factors_u = far_u[0]

    def project(block_index):
        first_col = column_ids[block_index] * block_width
        x_block = lax.dynamic_slice_in_dim(source, first_col, block_width, 1)
        return lax.switch(classes[block_index], project_fns, factors_v[block_index], x_block)

    coeffs = lax.map(project, jnp.arange(column_ids.shape[0], dtype=jnp.int32))
    rhs_count = coeffs.shape[2]

    def accumulate(running, packed):
        factor, coeff_block, level_id = packed
        return (lax.switch(level_id, expand_fns, running, factor, coeff_block), None)

    start_sum = jnp.zeros((rhs_count, cluster_size), jnp.float32)
    far_part = lax.scan(accumulate, start_sum, (factors_u, coeffs, classes))[0]
    combined = far_part + near_part
    return lax.psum_scatter(combined, "rhs", scatter_dimension=0, tiled=True).astype(jnp.bfloat16)


def solution(mesh):
    in_specs = (
        P("rhs", "rows"),
        P("rows", "rhs", None, None),
        P("rows", "rhs", None, None),
        P("rows", "rhs"),
        P("rows", "rhs"),
        P("rows", "rhs"),
    )
    out_specs = P("rhs", "rows")
    return jax.shard_map(
        on_device, mesh=mesh, in_specs=in_specs, out_specs=out_specs, check_vma=False
    )
```

profile of v0, /device:TPU:1, one launch (start us, length us, event | category | flops | bytes accessed | tf_op | source)
XLA Modules:
  0.0 294.4 jit_solution(12400122151808529447)
XLA Ops:
  6.5 17.5 %all_gather.6 = bf16[64,4096]{1,0:T(8,128)(2,1)} all-gather(bf16[8,4096]{1,0:T(8,128)(2,1)} %param.16), channel_id=1, replica_groups=mesh['rows'=32,'rhs'=8] {'rhs'}, dimensions={0}, use_global_device_ids=true | all-gather | bytes 589824 | tf_op jit(solution)/shard_map/all_gather | solution.py:35
  24.1 140.8 %all-gather.2.cloned.1.call-done = bf16[64,131072]{1,0:T(8,128)(2,1)} async-done(((bf16[64,4096]{1,0:T(8,128)(2,1)}), bf16[64,131072]{1,0:T(8,128)(2,1)}) %all-gather.2.cloned.1.call-update) | async-done | bytes 16777232 | tf_op jit(solution)/shard_map/all_gather | solution.py:36
  164.8 59.6 %while.20 = (s32[]{:T(128)}, bf16[8,64,64]{2,1,0:T(8,128)(2,1)S(1)}, s32[8]{0:T(128)S(1)}, s32[8]{0:T(128)}, s32[8]{0:T(128)}, /*index=5*/bf16[8,64,512]{2,1,0:T...) while((s32[]{:T(128)}, ...), condition=%wide.region_4.5_spmd, body=%wide.region_0.4_spmd.sunk | while | flops 4198410 | bytes 172849 | solution.py:52
  167.3 1.3 dynamic_slice.85
  169.2 1.3 dynamic_slice.84
  174.7 1.3 dynamic_slice.85
  182.2 1.3 dynamic_slice.85
  189.7 1.3 dynamic_slice.85
  197.1 1.3 dynamic_slice.85
  204.6 1.3 dynamic_slice.85
  212.0 1.3 dynamic_slice.85
  219.5 1.3 dynamic_slice.85
  224.6 27.3 %while.21 = (s32[]{:T(128)}, f32[64,4096]{1,0:T(8,128)S(1)}, s32[8]{0:T(128)}, bf16[8,64,4096]{2,1,0:T(8,128)(2,1)}, bf16[8,64,64]{2,1,0:T(8,128)(2,1)S(1)}, /*index=5*/s32[]{:T(128)}, s32[1]{0:T(128)}, s32[1]{0:T(128)}) while((s32[]{:T(128)}, f32[64,4096]{1,0:T(8,128)S(1)}, s32[8]{0:T(128)}, bf16[8,64,4096]{2,1,0:T(8,128)(2,1)}, ...), condition=%wide.region_9.10_spmd, body=%wide.region_5.9_spmd.sunk | while | flops 33816576 | bytes 3694745 | solution.py:60
  225.7 1.3 dynamic_slice.88
  229.1 1.3 dynamic_slice.88
  232.5 1.3 dynamic_slice.88
  235.9 1.3 dynamic_slice.88
  239.3 1.3 dynamic_slice.88
  242.7 1.3 dynamic_slice.88
  246.2 1.3 dynamic_slice.88
  249.6 1.3 dynamic_slice.88
  251.9 4.6 %convolution_add_fusion.3 = f32[64,4096]{1,0:T(8,128)} fusion(f32[64,4096]{1,0:T(8,128)S(1)} %get-tuple-element.226, bf16[4096,512]{1,0:T(8,128)(2,1)} %param.21, bf16[64,4096]{1,0:T(8,128)(2,1)} %all_gather.6, s32[]{:T(128)S(6)} %select_n.21), kind=kOutput, calls=%fused_computation.26 | convolution fusion | flops 268697600 | bytes 6356996 | tf_op jit(solution)/shard_map/ct,st->cs/dot_general | solution.py:41
  256.5 29.5 %reduce-scatter.2.cloned.1.call-done = f32[8,4096]{1,0:T(8,128)} async-done(((f32[64,4096]{1,0:T(8,128)}), f32[8,4096]{1,0:T(8,128)}) %reduce-scatter.2.cloned.1.call-update) | async-done | bytes 131088 | tf_op jit(solution)/shard_map/reduce_scatter | solution.py:62
  286.0 1.5 convert_element_type.19
  (78 shorter events, 47.1 us)
Async XLA Ops:
  6.5 158.3 %all-gather.2.cloned.1.call-start = ((), (), s32[]{:S(2)}) async-start(), calls=%async_computation.1 | async-start | bytes 17301504 | tf_op jit(solution)/shard_map/all_gather | solution.py:36
  24.0 261.9 %reduce-scatter.2.cloned.1.call-start = ((), (), s32[]{:S(2)}) async-start(), calls=%async_computation.2 | async-start | bytes 1179648 | tf_op jit(solution)/shard_map/reduce_scatter | solution.py:62
Sparse Core Ops, SparseCore 0:
  24.1 140.6 all-gather.1
  256.6 29.3 reduce-scatter.1
where the time goes:
time: 297 us; the launch traced here: 294 us
  waiting for transfers between devices  170 us (57%)
  local copies, waits for them, and re-layouts  44.6 us (15%)
  loops' own time  30.6 us (10%)
  blocking collectives  17.5 us (6%)
  matrix products  16.4 us (6%)
  between operations  13.4 us (5%)
    all_gather x1, waiting for transfers between devices, on_device(): source = lax.all_gather(own_block, 'rows', axis=1, tiled=True)  141 us
    reduce_scatter x1, waiting for transfers between devices, on_device(): lax.psum_scatter(combined, 'rhs', scatter_dimension=0, tiled=True)  29.5 us
    another operation x1, loops' own time, on_device(): coeffs = lax.map(project, jnp.arange(column_ids.shape[0], dtype=jnp.int32))  24.6 us
    all_gather x1, blocking collectives, on_device(): own_block = lax.all_gather(x_t, 'rhs', axis=0, tiled=True)  17.5 us
    dynamic_slice x16, local copies, waits for them, and re-layouts, on_device(): coeffs = lax.map(project, jnp.arange(column_ids.shape[0], dtype=jnp.int32))  15.3 us
    dynamic_slice x8, local copies, waits for them, and re-layouts, project(): first_col = column_ids[block_index] * block_width  10.2 us
    dynamic_slice x8, local copies, waits for them, and re-layouts, project(): classes[block_index]  10.2 us
    dot_general x8, matrix products, low_branch(): jnp.einsum('rt,ct->rc', factor[:rank_cut], x_block, preferred_element_typ...  9.23 us
  transfers between devices with their start and end apart: 2, of which 2 were waited for; matrix products, arithmetic and copies ran while one was open for 0% of the time, Pallas kernels for 0%

commit v1 on v0

v1 whole, which is shorter than its diff:
```python
import jax
import jax.numpy as jnp
from jax import lax
from jax.experimental import pallas as pl
from jax.experimental.pallas import tpu as pltpu
from jax.sharding import PartitionSpec as P

Z, Y, X, C = 8, 4, 4, 2
PIECES, BLK, RANK, W, S = 8, 8, 64, 512, 4096
AXES = ("rows", "rhs")
NT = (((1,), (1,)), ((), ()))
NN = (((1,), (0,)), ((), ()))
TILE = 512
VMEM, SMEM = pl.BlockSpec(memory_space=pltpu.VMEM), pl.BlockSpec(memory_space=pltpu.SMEM)
ORDER = (5, 3, 4, 6, 2, 7, 1, 0)
LONG = pl.CostEstimate(flops=20 << 30, bytes_accessed=1 << 20, transcendentals=0)
LIMIT = pltpu.CompilerParams(vmem_limit_bytes=8 << 20)


def bf16(*shape):
    return jax.ShapeDtypeStruct(shape, jnp.bfloat16)


def f32(*shape):
    return jax.ShapeDtypeStruct(shape, jnp.float32)


def pairs(target):
    place = lambda z, y, x, c: ((z * Y + y) * X + x) * C + c
    return [
        (place(z, y, x, c), place(*target(z, y, x, c)))
        for z in range(Z) for y in range(Y) for x in range(X) for c in range(C)
    ]


def move(part, target):
    return lax.ppermute(part, AXES, pairs(target))


def along_x(part, m):
    return part if m == 0 else move(part, lambda z, y, x, c: (z, y, (x + m) % X, c))


def along_y(part, m):
    return part if m == 0 else move(part, lambda z, y, x, c: (z, (y + m) % Y, x, c))


def along_z(part, m):
    return part if m == 0 else move(part, lambda z, y, x, c: ((z + m) % Z, y, x, c))


def other_core(part):
    return move(part, lambda z, y, x, c: (z, y, x, 1 - c))


def pick_kernel(*refs):
    held_refs, table_ref, out_refs, held_ref = refs[:Y], refs[Y], refs[Y + 1:-1], refs[-1]
    y, z = lax.axis_index("rows") & 3, lax.axis_index("rows") >> 2
    for m in range(Y):
        held_ref[m] = held_refs[m][...]
    for m in range(Z):
        for b in range(BLK):
            piece = table_ref[(z + m) & 7, 0, b]
            source = (y - (piece >> 3)) & 3
            out_refs[m][b] = held_ref[source, :, pl.ds(pl.multiple_of((piece & 7) * W, W), W)]


def pick(table, held):
    return pl.pallas_call(
        pick_kernel,
        out_shape=[bf16(BLK, 8, W)] * Z,
        in_specs=[VMEM] * Y + [SMEM],
        out_specs=[VMEM] * Z,
        scratch_shapes=[pltpu.VMEM((Y, 8, PIECES * W), jnp.bfloat16)],
        compiler_params=LIMIT,
        cost_estimate=LONG,
        name="pick",
    )(*held, table)


def halves_kernel(cols_ref, x_ref, table_ref, mine_ref, yours_ref):
    table_ref[...] = jnp.zeros_like(table_ref)
    table_ref[:, :, :BLK] = jnp.broadcast_to(cols_ref[...], (Z, 1, BLK))
    k = lax.axis_index("rhs")
    x, core = k >> 1, k & 1
    for m in range(X):
        for c, ref in ((core, mine_ref), (1 - core, yours_ref)):
            start = pl.multiple_of((((x + m) & 3) * 2 + c) * W, W)
            ref[m] = x_ref[:, pl.ds(start, W)]


def halves(far_cols, x_t):
    return pl.pallas_call(
        halves_kernel,
        out_shape=[jax.ShapeDtypeStruct((Z, 1, 128), jnp.int32)] + [bf16(X, 8, W)] * 2,
        in_specs=[VMEM] * 2,
        out_specs=[VMEM] * 3,
        compiler_params=LIMIT,
        cost_estimate=LONG,
        name="halves",
    )(far_cols, x_t)


def own_piece(mine, yours):
    theirs = other_core(yours)
    parts = [along_x(jnp.stack([mine[m], theirs[m]]), m) for m in range(X)]
    return [parts[-p % X] for p in range(X)]


def product_kernel(cls_ref, *refs):
    got_refs, own_refs, (v_ref, near_ref, u_ref, keep_ref, send_ref, z_buf) = refs[:Z], refs[Z:Z + X], refs[Z + X:]
    k, depth = lax.axis_index("rhs"), lax.axis_index("rows") >> 2
    x, core = k >> 1, k & 1
    got = [got_refs[ORDER.index(m)] for m in range(Z)]
    ranks = lax.broadcasted_iota(jnp.int32, (64, RANK), 1)
    halves = []
    for b in range(BLK):
        block = jnp.concatenate([r[b].astype(jnp.float32) for r in got], 0).astype(jnp.bfloat16)
        z = lax.dot_general(block, v_ref[b], NT, preferred_element_type=jnp.float32)
        rank = jnp.where(cls_ref[b] == 0, RANK // 4, jnp.where(cls_ref[b] == 1, RANK // 2, RANK))
        halves.append(jnp.where(ranks < rank, z, 0.0))
    for b in range(0, BLK, 2):
        z_buf[b // 2] = jnp.concatenate(halves[b:b + 2], 1).reshape(8, 8, 2 * RANK)
    order = [((x + p) & 3) * 2 + core for p in range(X)] + [((x + p) & 3) * 2 + 1 - core for p in range(X)]
    zmask = jnp.concatenate(
        [jnp.concatenate([z_buf[j, (depth - place) & 7] for place in order], 0) for j in range(BLK // 2)], 1
    ).astype(jnp.bfloat16)
    own = jnp.concatenate([r[c].astype(jnp.float32) for c in range(C) for r in own_refs], 0).astype(jnp.bfloat16)
    for t in range(0, S, TILE):
        cols = slice(t, t + TILE)
        y = lax.dot_general(own, near_ref[cols, :], NT, preferred_element_type=jnp.float32)
        y += lax.dot_general(zmask, u_ref[:, cols], NN, preferred_element_type=jnp.float32)
        keep_ref[:, cols] = y[:32]
        send_ref[:, cols] = y[32:].astype(jnp.bfloat16)


def product(classes, got, own, v, near, u):
    return pl.pallas_call(
        product_kernel,
        out_shape=(f32(32, S), bf16(32, S)),
        in_specs=[SMEM] + [VMEM] * (Z + X + 3),
        out_specs=(VMEM, VMEM),
        scratch_shapes=[pltpu.VMEM((BLK // 2, 8, 8, 2 * RANK), jnp.float32)],
        compiler_params=LIMIT,
        cost_estimate=pl.CostEstimate(flops=4 * 64 * W * S, bytes_accessed=10 << 20, transcendentals=0),
        name="product",
    )(classes, *got, *own, v, near, u)


def on_device(x_t, far_v, far_u, far_cols, rank_class, near_block):
    asked, kept, given = halves(far_cols, x_t)
    mine = move(x_t, lambda z, y, x, c: (2 * x + c, y, z // 2, z % 2))
    lines = [[z * Y + y for z in range(Z)] for y in range(Y)]
    table = lax.all_to_all(asked, "rows", 0, 0, axis_index_groups=lines, tiled=True)
    mine, table = lax.optimization_barrier((mine, table))
    sent = pick(table, [along_y(mine, m) for m in range(Y)])
    own = own_piece(kept, given)
    got = [along_z(sent[m], m) for m in ORDER]
    keep, send = product(
        rank_class.reshape(BLK), got, own, far_v.reshape(BLK, RANK, W), near_block, far_u.reshape(BLK * RANK, S)
    )
    both = keep + other_core(send).astype(jnp.float32)
    parts = [along_x(both[8 * m:8 * m + 8].astype(jnp.bfloat16), m) for m in (2, 1, 3)]
    total = both[:8]
    for part in parts:
        total = total + part.astype(jnp.float32)
    return total.astype(jnp.bfloat16)


def solution(mesh):
    in_specs = (
        P("rhs", "rows"),
        P("rows", "rhs", None, None),
        P("rows", "rhs", None, None),
        P("rows", "rhs"),
        P("rows", "rhs"),
        P("rows", "rhs"),
    )
    return jax.shard_map(on_device, mesh=mesh, in_specs=in_specs, out_specs=P("rhs", "rows"), check_vma=False)
```

time: 297 us -> 66.5 us (0.22)
  waiting for transfers between devices: 170 us -> 14 us
  starting transfers between devices: 0.04 us -> 45.6 us
  local copies, waits for them, and re-layouts: 44.6 us -> 1.54 us
  loops' own time: 30.6 us -> 0 us
  blocking collectives: 17.5 us -> 0 us
  matrix products: 16.4 us -> 0 us
  between operations: 13.4 us -> 0.1 us
  Pallas kernels: 0 us -> 4.38 us
    all_gather x1 -> x0, waiting for transfers between devices: 141 us -> none  [on_device(): source = lax.all_gather(own_block, 'rows', axis=1, tiled=True)]
    ppermute x0 -> x19, starting transfers between devices: none -> 37.6 us  [move(): return lax.ppermute(part, AXES, pairs(target))]
    dynamic_slice x32 -> x0, local copies, waits for them, and re-layouts: 35.7 us -> none  [the longest x16 15.3 us: on_device(): coeffs = lax.map(project, jnp.arange(column_ids.shape[0], dtype=jnp.int32))]
    another operation x18 -> x0, loops' own time: 30.6 us -> none  [the longest x1 24.6 us: on_device(): coeffs = lax.map(project, jnp.arange(column_ids.shape[0], dtype=jnp.int32))]
    reduce_scatter x1 -> x0, waiting for transfers between devices: 29.5 us -> none  [on_device(): lax.psum_scatter(combined, 'rhs', scatter_dimension=0, tiled=True)]
    all_gather x1 -> x0, blocking collectives: 17.5 us -> none  [on_device(): own_block = lax.all_gather(x_t, 'rhs', axis=0, tiled=True)]
    dot_general x17 -> x0, matrix products: 16.4 us -> none  [the longest x8 9.23 us: low_branch(): jnp.einsum('rt,ct->rc', factor[:rank_cut], x_block, preferred_element_typ...]
    ppermute x0 -> x19, waiting for transfers between devices: none -> 12.2 us  [move(): return lax.ppermute(part, AXES, pairs(target))]
  transfers between devices with their start and end apart: 2 -> 20, of which waited for: 2 -> 11; matrix products, arithmetic and copies ran while one was open for 0% -> 0% of each run, Pallas kernels for 0% -> 2%
where the time goes in v1:
time: 66.5 us; the launch traced here: 66.3 us
  starting transfers between devices  45.6 us (69%)
  waiting for transfers between devices  14 us (21%)
  Pallas kernels  4.38 us (7%)
  local copies, waits for them, and re-layouts  1.54 us (2%)
  other arithmetic  0.73 us (1%)
    ppermute x19, starting transfers between devices, move(): return lax.ppermute(part, AXES, pairs(target))  37.6 us
    ppermute x19, waiting for transfers between devices, move(): return lax.ppermute(part, AXES, pairs(target))  12.2 us
    all_to_all x1, starting transfers between devices, on_device(): lax.all_to_all(asked, 'rows', 0, 0, axis_index_groups=lines, tiled=True)  7.93 us
    pallas_call x1, Pallas kernels, product(): pl.pallas_call(product_kernel, out_shape=(f32(32, S), bf16(32, S)), in_sp...  2.96 us
    all_to_all x1, waiting for transfers between devices, on_device(): lax.all_to_all(asked, 'rows', 0, 0, axis_index_groups=lines, tiled=True)  1.77 us
    unnamed x12, local copies, waits for them, and re-layouts  1.52 us
  transfers between devices with their start and end apart: 20, of which 11 were waited for; matrix products, arithmetic and copies ran while one was open for 0% of the time, Pallas kernels for 2%

profile of v1, /device:TPU:1, one launch (start us, length us, event | category | flops | bytes accessed | tf_op | source)
XLA Modules:
  0.0 66.3 jit_solution(9875037758759007885)
XLA Ops:
  0.0 4.9 %collective-permute-start = (bf16[8,4096]{1,0:T(8,128)(2,1)}, bf16[8,4096]{1,0:T(8,128)(2,1)S(1)}, u32[]{:S(2)}, u32[]{:S(2)}) collective-permute-start(bf16[8,4096]{1,0:T(8,128)(2,1)} %x_ref.1), channel_id=1, source_target_pairs={{0,0},{1,32},{2,64},{3,96},{4,128},{5,160},{6,192},{7,224},{8,8},{... | collective-permute-start | bytes 196616 | tf_op jit(solution)/shard_map/ppermute | solution.py:37
  4.9 0.8 %copy-done.4 = bf16[8,4096]{1,0:T(8,128)(2,1)S(1)} copy-done((bf16[8,4096]{1,0:T(8,128)(2,1)S(1)}, bf16[8,4096]{1,0:T(8,128)(2,1)}, u32[]{:S(2)}) %copy-start.4) | copy-done | bytes 65560
  7.0 7.9 %all-to-all-start = ((s32[8,1,128]{2,1,0:T(1,128)}), s32[8,1,128]{2,1,0:T(1,128)S(1)}, u32[]{:S(2)}, u32[]{:S(2)}) async-start(s32[8,1,128]{2,1,0:T(1,128)} %get-tuple-element.20), calls=%async_computation | async-start | bytes 8192 | tf_op jit(solution)/shard_map/all_to_all | solution.py:154
  15.2 1.0 %collective-permute-done.11 = bf16[4,8,512]{2,1,0:T(8,128)(2,1)S(1)} collective-permute-done((bf16[4,8,512]{2,1,0:T(8,128)(2,1)S(1)}, bf16[4,8,512]{2,1,0:T(8,128)(2,1)S(1)}, u32[]{:S(2)}, u32[]{:S(2)}) %collective-permute-start.11) | collective-permute-done | bytes 32800 | tf_op jit(solution)/shard_map/ppermute | solution.py:37
  16.2 3.5 %collective-permute-start.12 = (bf16[2,8,512]{2,1,0:T(8,128)(2,1)S(1)}, bf16[2,8,512]{2,1,0:T(8,128)(2,1)S(1)}, u32[]{:S(2)}, u32[]{:S(2)}) collective-permute-start(bf16[2,8,512]{2,1,0:T(8,128)(2,1)S(1)} %pad_maximum_fusion.1), channel_id=1, source_target_pairs={{0,6},{1,7},{2,0},{3,1},{4,2},{5,3},{6,4},{7,5},{8,14},{9,15},{10,... | collective-permute-start | bytes 49160 | tf_op jit(solution)/shard_map/ppermute | solution.py:37
  19.6 1.8 %all-to-all-done.refs_4_ = s32[8,1,128]{2,1,0:T(1,128)S(1)} async-done(((s32[8,1,128]{2,1,0:T(1,128)}), s32[8,1,128]{2,1,0:T(1,128)S(1)}, u32[]{:S(2)}, u32[]{:S(2)}) %all-to-all-start) | async-done | bytes 4128 | tf_op jit(solution)/shard_map/all_to_all | solution.py:154
  21.4 2.7 %collective-permute-start.3 = (bf16[8,4096]{1,0:T(8,128)(2,1)S(1)}, bf16[8,4096]{1,0:T(8,128)(2,1)S(1)}, u32[]{:S(2)}, u32[]{:S(2)}) collective-permute-start(bf16[8,4096]{1,0:T(8,128)(2,1)S(1)} %collective-permute-done.refs_0_), channel_id=1, source_target_pairs={{0,24},{1,25},{2,26},{3,27},{4,28},{5,29},{6,30},{7,31},{8,0},{9,1... | collective-permute-start | bytes 196616 | tf_op jit(solution)/shard_map/ppermute | solution.py:37
  25.2 2.9 %collective-permute-start.13 = (bf16[2,8,512]{2,1,0:T(8,128)(2,1)S(1)}, bf16[2,8,512]{2,1,0:T(8,128)(2,1)S(1)}, u32[]{:S(2)}, u32[]{:S(2)}) collective-permute-start(bf16[2,8,512]{2,1,0:T(8,128)(2,1)S(1)} %pad_maximum_fusion.2), channel_id=1, source_target_pairs={{0,4},{1,5},{2,6},{3,7},{4,0},{5,1},{6,2},{7,3},{8,12},{9,13},{10,... | collective-permute-start | bytes 49160 | tf_op jit(solution)/shard_map/ppermute | solution.py:37
  29.5 0.8 %pick.1 = (bf16[8,8,512]{2,1,0:T(8,128)(2,1)S(1)}, bf16[8,8,512]{2,1,0:T(8,128)(2,1)S(1)}, bf16[8,8,512]{2,1,0:T(8,128)(2,1)S(1)}, bf16[8,8,512]{2,1,0:T(8,128)(...) custom-call(bf16[8,4096]{1,0:T(8,128)(2,1)S(1)} %collective-permute-, ...), custom_call_target="tpu_custom_call" | custom-call | flops 21474836480 | bytes 1048576 | tf_op jit(solution)/shard_map/pick/pallas_call | solution.py:69
  30.3 3.1 %collective-permute-start.4 = (bf16[8,8,512]{2,1,0:T(8,128)(2,1)S(1)}, bf16[8,8,512]{2,1,0:T(8,128)(2,1)S(1)}, u32[]{:S(2)}, u32[]{:S(2)}) collective-permute-start(bf16[8,8,512]{2,1,0:T(8,128)(2,1)S(1)} %get-tuple-element.23), channel_id=1, source_target_pairs={{0,160},{1,161},{2,162},{3,163},{4,164},{5,165},{6,166},{7,167},{8... | collective-permute-start | bytes 196616 | tf_op jit(solution)/shard_map/ppermute | solution.py:37
  33.7 1.2 %collective-permute-start.14 = (bf16[2,8,512]{2,1,0:T(8,128)(2,1)S(1)}, bf16[2,8,512]{2,1,0:T(8,128)(2,1)S(1)}, u32[]{:S(2)}, u32[]{:S(2)}) collective-permute-start(bf16[2,8,512]{2,1,0:T(8,128)(2,1)S(1)} %pad_maximum_fusion.3), channel_id=1, source_target_pairs={{0,2},{1,3},{2,4},{3,5},{4,6},{5,7},{6,0},{7,1},{8,10},{9,11},{10,... | collective-permute-start | bytes 49160 | tf_op jit(solution)/shard_map/ppermute | solution.py:37
  34.9 2.8 %collective-permute-start.6 = (bf16[8,8,512]{2,1,0:T(8,128)(2,1)S(1)}, bf16[8,8,512]{2,1,0:T(8,128)(2,1)S(1)}, u32[]{:S(2)}, u32[]{:S(2)}) collective-permute-start(bf16[8,8,512]{2,1,0:T(8,128)(2,1)S(1)} %get-tuple-element.25), channel_id=1, source_target_pairs={{0,128},{1,129},{2,130},{3,131},{4,132},{5,133},{6,134},{7,135},{8... | collective-permute-start | bytes 196616 | tf_op jit(solution)/shard_map/ppermute | solution.py:37
  37.6 2.0 %collective-permute-start.7 = (bf16[8,8,512]{2,1,0:T(8,128)(2,1)S(1)}, bf16[8,8,512]{2,1,0:T(8,128)(2,1)S(1)}, u32[]{:S(2)}, u32[]{:S(2)}) collective-permute-start(bf16[8,8,512]{2,1,0:T(8,128)(2,1)S(1)} %get-tuple-element.26), channel_id=1, source_target_pairs={{0,192},{1,193},{2,194},{3,195},{4,196},{5,197},{6,198},{7,199},{8... | collective-permute-start | bytes 196616 | tf_op jit(solution)/shard_map/ppermute | solution.py:37
  40.0 2.7 %collective-permute-start.9 = (bf16[8,8,512]{2,1,0:T(8,128)(2,1)S(1)}, bf16[8,8,512]{2,1,0:T(8,128)(2,1)S(1)}, u32[]{:S(2)}, u32[]{:S(2)}) collective-permute-start(bf16[8,8,512]{2,1,0:T(8,128)(2,1)S(1)} %get-tuple-element.28), channel_id=1, source_target_pairs={{0,224},{1,225},{2,226},{3,227},{4,228},{5,229},{6,230},{7,231},{8... | collective-permute-start | bytes 196616 | tf_op jit(solution)/shard_map/ppermute | solution.py:37
  42.7 1.9 %collective-permute-done.6.refs_2_ = bf16[8,8,512]{2,1,0:T(8,128)(2,1)S(1)} collective-permute-done((bf16[8,8,512]{2,1,0:T(8,128)(2,1)S(1)}, bf16[8,8,512]{2,1,0:T(8,128)(2,1)S(1)}, u32[]{:S(2)}, u32[]{:S(2)}) %collective-permute-start.6) | collective-permute-done | bytes 65568 | tf_op jit(solution)/shard_map/ppermute | solution.py:37
  44.7 2.0 %collective-permute-done.8.refs_4_ = bf16[8,8,512]{2,1,0:T(8,128)(2,1)S(1)} collective-permute-done((bf16[8,8,512]{2,1,0:T(8,128)(2,1)S(1)}, bf16[8,8,512]{2,1,0:T(8,128)(2,1)S(1)}, u32[]{:S(2)}, u32[]{:S(2)}) %collective-permute-start.8) | collective-permute-done | bytes 65568 | tf_op jit(solution)/shard_map/ppermute | solution.py:37
  46.7 1.2 %collective-permute-done.10.refs_6_ = bf16[8,8,512]{2,1,0:T(8,128)(2,1)S(1)} collective-permute-done((bf16[8,8,512]{2,1,0:T(8,128)(2,1)S(1)}, bf16[8,8,512]{2,1,0:T(8,128)(2,1)S(1)}, u32[]{:S(2)}, u32[]{:S(2)}) %collective-permute-start.10) | collective-permute-done | bytes 65568 | tf_op jit(solution)/shard_map/ppermute | solution.py:37
  47.9 3.0 %product.1 = (f32[32,4096]{1,0:T(8,128)S(1)}, bf16[32,4096]{1,0:T(8,128)(2,1)S(1)}) custom-call(s32[8]{0:T(128)S(1)} %bitcast.5, bf16[8,8,512]{2,1,0:T(8,128)(2,1)S(1)} %collective-permute-done.4.refs_0_, bf16[8,8,512]{2,1,0:T(8,128)(2,1)S(1)} %collective-permute-done.5.refs_1_, bf16[8,8,512]{2,1,0:T(8,128)(2,1)S(1)} %collective-permute-done.6.refs_2_, ...), custom_call_target="tpu_custom_call" | custom-call | flops 536870912 | bytes 10485760 | tf_op jit(solution)/shard_map/product/pallas_call | solution.py:138
  50.8 4.8 %collective-permute-start.15 = (bf16[32,4096]{1,0:T(8,128)(2,1)S(1)}, bf16[32,4096]{1,0:T(8,128)(2,1)S(1)}, u32[]{:S(2)}, u32[]{:S(2)}) collective-permute-start(bf16[32,4096]{1,0:T(8,128)(2,1)S(1)} %get-tuple-element.34), channel_id=1, source_target_pairs={{0,1},{1,0},{2,3},{3,2},{4,5},{5,4},{6,7},{7,6},{8,9},{9,8},{10,11... | collective-permute-start | bytes 786440 | tf_op jit(solution)/shard_map/ppermute | solution.py:37
  55.7 1.2 %collective-permute-done.15 = bf16[32,4096]{1,0:T(8,128)(2,1)S(1)} collective-permute-done((bf16[32,4096]{1,0:T(8,128)(2,1)S(1)}, bf16[32,4096]{1,0:T(8,128)(2,1)S(1)}, u32[]{:S(2)}, u32[]{:S(2)}) %collective-permute-start.15) | collective-permute-done | bytes 262176 | tf_op jit(solution)/shard_map/ppermute | solution.py:37
  56.9 3.6 %collective-permute-start.16 = (bf16[8,4096]{1,0:T(8,128)(2,1)S(1)}, bf16[8,4096]{1,0:T(8,128)(2,1)S(1)}, u32[]{:S(2)}, u32[]{:S(2)}) collective-permute-start(bf16[8,4096]{1,0:T(8,128)(2,1)S(1)} %get-tuple-element.37), channel_id=1, source_target_pairs={{0,4},{1,5},{2,6},{3,7},{4,0},{5,1},{6,2},{7,3},{8,12},{9,13},{10,... | collective-permute-start | bytes 196616 | tf_op jit(solution)/shard_map/ppermute | solution.py:37
  60.6 0.7 %collective-permute-start.18 = (bf16[8,4096]{1,0:T(8,128)(2,1)S(1)}, bf16[8,4096]{1,0:T(8,128)(2,1)S(1)}, u32[]{:S(2)}, u32[]{:S(2)}) collective-permute-start(bf16[8,4096]{1,0:T(8,128)(2,1)S(1)} %get-tuple-element.38), channel_id=1, source_target_pairs={{0,6},{1,7},{2,0},{3,1},{4,2},{5,3},{6,4},{7,5},{8,14},{9,15},{10,... | collective-permute-start | bytes 196616 | tf_op jit(solution)/shard_map/ppermute | solution.py:37
  62.7 1.0 %collective-permute-done.18 = bf16[8,4096]{1,0:T(8,128)(2,1)S(1)} collective-permute-done((bf16[8,4096]{1,0:T(8,128)(2,1)S(1)}, bf16[8,4096]{1,0:T(8,128)(2,1)S(1)}, u32[]{:S(2)}, u32[]{:S(2)}) %collective-permute-start.18) | collective-permute-done | bytes 65568 | tf_op jit(solution)/shard_map/ppermute | solution.py:37
  63.7 2.0 %collective-permute-done.17 = bf16[8,4096]{1,0:T(8,128)(2,1)S(1)} collective-permute-done((bf16[8,4096]{1,0:T(8,128)(2,1)S(1)}, bf16[8,4096]{1,0:T(8,128)(2,1)S(1)}, u32[]{:S(2)}, u32[]{:S(2)}) %collective-permute-start.17) | collective-permute-done | bytes 65568 | tf_op jit(solution)/shard_map/ppermute | solution.py:37
  (40 shorter events, 6.7 us)
Async XLA Ops:
  0.0 21.4 %collective-permute-start = (bf16[8,4096]{1,0:T(8,128)(2,1)}, bf16[8,4096]{1,0:T(8,128)(2,1)S(1)}, u32[]{:S(2)}, u32[]{:S(2)}) collective-permute-start(bf16[8,4096]{1,0:T(8,128)(2,1)} %x_ref.1), channel_id=1, source_target_pairs={{0,0},{1,32},{2,64},{3,96},{4,128},{5,160},{6,192},{7,224},{8,8},{... | collective-permute-start | bytes 196616 | tf_op jit(solution)/shard_map/ppermute | solution.py:37
  7.0 14.4 %all-to-all-start = ((s32[8,1,128]{2,1,0:T(1,128)}), s32[8,1,128]{2,1,0:T(1,128)S(1)}, u32[]{:S(2)}, u32[]{:S(2)}) async-start(s32[8,1,128]{2,1,0:T(1,128)} %get-tuple-element.20), calls=%async_computation | async-start | bytes 8192 | tf_op jit(solution)/shard_map/all_to_all | solution.py:154
  15.0 1.2 %collective-permute-start.11 = (bf16[4,8,512]{2,1,0:T(8,128)(2,1)S(1)}, bf16[4,8,512]{2,1,0:T(8,128)(2,1)S(1)}, u32[]{:S(2)}, u32[]{:S(2)}) collective-permute-start(bf16[4,8,512]{2,1,0:T(8,128)(2,1)S(1)} %get-tuple-element.32), channel_id=1, source_target_pairs={{0,1},{1,0},{2,3},{3,2},{4,5},{5,4},{6,7},{7,6},{8,9},{9,8},{10,11... | collective-permute-start | bytes 98312 | tf_op jit(solution)/shard_map/ppermute | solution.py:37
  16.2 18.7 %collective-permute-start.12 = (bf16[2,8,512]{2,1,0:T(8,128)(2,1)S(1)}, bf16[2,8,512]{2,1,0:T(8,128)(2,1)S(1)}, u32[]{:S(2)}, u32[]{:S(2)}) collective-permute-start(bf16[2,8,512]{2,1,0:T(8,128)(2,1)S(1)} %pad_maximum_fusion.1), channel_id=1, source_target_pairs={{0,6},{1,7},{2,0},{3,1},{4,2},{5,3},{6,4},{7,5},{8,14},{9,15},{10,... | collective-permute-start | bytes 49160 | tf_op jit(solution)/shard_map/ppermute | solution.py:37
  21.4 6.7 %collective-permute-start.3 = (bf16[8,4096]{1,0:T(8,128)(2,1)S(1)}, bf16[8,4096]{1,0:T(8,128)(2,1)S(1)}, u32[]{:S(2)}, u32[]{:S(2)}) collective-permute-start(bf16[8,4096]{1,0:T(8,128)(2,1)S(1)} %collective-permute-done.refs_0_), channel_id=1, source_target_pairs={{0,24},{1,25},{2,26},{3,27},{4,28},{5,29},{6,30},{7,31},{8,0},{9,1... | collective-permute-start | bytes 196616 | tf_op jit(solution)/shard_map/ppermute | solution.py:37
  24.2 4.7 %collective-permute-start.2 = (bf16[8,4096]{1,0:T(8,128)(2,1)S(1)}, bf16[8,4096]{1,0:T(8,128)(2,1)S(1)}, u32[]{:S(2)}, u32[]{:S(2)}) collective-permute-start(bf16[8,4096]{1,0:T(8,128)(2,1)S(1)} %collective-permute-done.refs_0_), channel_id=1, source_target_pairs={{0,16},{1,17},{2,18},{3,19},{4,20},{5,21},{6,22},{7,23},{8,24},{9,... | collective-permute-start | bytes 196616 | tf_op jit(solution)/shard_map/ppermute | solution.py:37
  24.5 5.0 %collective-permute-start.1 = (bf16[8,4096]{1,0:T(8,128)(2,1)S(1)}, bf16[8,4096]{1,0:T(8,128)(2,1)S(1)}, u32[]{:S(2)}, u32[]{:S(2)}) collective-permute-start(bf16[8,4096]{1,0:T(8,128)(2,1)S(1)} %collective-permute-done.refs_0_), channel_id=1, source_target_pairs={{0,8},{1,9},{2,10},{3,11},{4,12},{5,13},{6,14},{7,15},{8,16},{9,17... | collective-permute-start | bytes 196616 | tf_op jit(solution)/shard_map/ppermute | solution.py:37
  25.2 22.6 %copy-start = (bf16[4096,512]{1,0:T(8,128)(2,1)S(1)}, bf16[4096,512]{1,0:T(8,128)(2,1)}, u32[]{:S(2)}) copy-start(bf16[4096,512]{1,0:T(8,128)(2,1)} %refs_13_.1) | copy-start | bytes 12582916
  25.2 22.6 %copy-start.1 = (bf16[1,8,64,4096]{3,2,1,0:T(8,128)(2,1)S(1)}, bf16[1,8,64,4096]{3,2,1,0:T(8,128)(2,1)}, u32[]{:S(2)}) copy-start(bf16[1,8,64,4096]{3,2,1,0:T(8,128)(2,1)} %param.8) | copy-start | bytes 12582916
  25.2 22.7 %copy-start.2 = (bf16[1,8,64,512]{3,2,1,0:T(8,128)(2,1)S(1)}, bf16[1,8,64,512]{3,2,1,0:T(8,128)(2,1)}, u32[]{:S(2)}) copy-start(bf16[1,8,64,512]{3,2,1,0:T(8,128)(2,1)} %param.7) | copy-start | bytes 1572868
  25.2 22.6 %copy-start.3 = (s32[1,8]{1,0:T(1,128)S(1)}, s32[1,8]{1,0:T(1,128)}, u32[]{:S(2)}) copy-start(s32[1,8]{1,0:T(1,128)} %param.10) | copy-start | bytes 100
  25.2 12.4 %collective-permute-start.13 = (bf16[2,8,512]{2,1,0:T(8,128)(2,1)S(1)}, bf16[2,8,512]{2,1,0:T(8,128)(2,1)S(1)}, u32[]{:S(2)}, u32[]{:S(2)}) collective-permute-start(bf16[2,8,512]{2,1,0:T(8,128)(2,1)S(1)} %pad_maximum_fusion.2), channel_id=1, source_target_pairs={{0,4},{1,5},{2,6},{3,7},{4,0},{5,1},{6,2},{7,3},{8,12},{9,13},{10,... | collective-permute-start | bytes 49160 | tf_op jit(solution)/shard_map/ppermute | solution.py:37
  30.3 9.7 %collective-permute-start.4 = (bf16[8,8,512]{2,1,0:T(8,128)(2,1)S(1)}, bf16[8,8,512]{2,1,0:T(8,128)(2,1)S(1)}, u32[]{:S(2)}, u32[]{:S(2)}) collective-permute-start(bf16[8,8,512]{2,1,0:T(8,128)(2,1)S(1)} %get-tuple-element.23), channel_id=1, source_target_pairs={{0,160},{1,161},{2,162},{3,163},{4,164},{5,165},{6,166},{7,167},{8... | collective-permute-start | bytes 196616 | tf_op jit(solution)/shard_map/ppermute | solution.py:37
  33.4 9.3 %collective-permute-start.5 = (bf16[8,8,512]{2,1,0:T(8,128)(2,1)S(1)}, bf16[8,8,512]{2,1,0:T(8,128)(2,1)S(1)}, u32[]{:S(2)}, u32[]{:S(2)}) collective-permute-start(bf16[8,8,512]{2,1,0:T(8,128)(2,1)S(1)} %get-tuple-element.24), channel_id=1, source_target_pairs={{0,96},{1,97},{2,98},{3,99},{4,100},{5,101},{6,102},{7,103},{8,104... | collective-permute-start | bytes 196616 | tf_op jit(solution)/shard_map/ppermute | solution.py:37
  33.7 6.0 %collective-permute-start.14 = (bf16[2,8,512]{2,1,0:T(8,128)(2,1)S(1)}, bf16[2,8,512]{2,1,0:T(8,128)(2,1)S(1)}, u32[]{:S(2)}, u32[]{:S(2)}) collective-permute-start(bf16[2,8,512]{2,1,0:T(8,128)(2,1)S(1)} %pad_maximum_fusion.3), channel_id=1, source_target_pairs={{0,2},{1,3},{2,4},{3,5},{4,6},{5,7},{6,0},{7,1},{8,10},{9,11},{10,... | collective-permute-start | bytes 49160 | tf_op jit(solution)/shard_map/ppermute | solution.py:37
  34.9 9.8 %collective-permute-start.6 = (bf16[8,8,512]{2,1,0:T(8,128)(2,1)S(1)}, bf16[8,8,512]{2,1,0:T(8,128)(2,1)S(1)}, u32[]{:S(2)}, u32[]{:S(2)}) collective-permute-start(bf16[8,8,512]{2,1,0:T(8,128)(2,1)S(1)} %get-tuple-element.25), channel_id=1, source_target_pairs={{0,128},{1,129},{2,130},{3,131},{4,132},{5,133},{6,134},{7,135},{8... | collective-permute-start | bytes 196616 | tf_op jit(solution)/shard_map/ppermute | solution.py:37
  37.6 7.0 %collective-permute-start.7 = (bf16[8,8,512]{2,1,0:T(8,128)(2,1)S(1)}, bf16[8,8,512]{2,1,0:T(8,128)(2,1)S(1)}, u32[]{:S(2)}, u32[]{:S(2)}) collective-permute-start(bf16[8,8,512]{2,1,0:T(8,128)(2,1)S(1)} %get-tuple-element.26), channel_id=1, source_target_pairs={{0,192},{1,193},{2,194},{3,195},{4,196},{5,197},{6,198},{7,199},{8... | collective-permute-start | bytes 196616 | tf_op jit(solution)/shard_map/ppermute | solution.py:37
  39.7 7.0 %collective-permute-start.8 = (bf16[8,8,512]{2,1,0:T(8,128)(2,1)S(1)}, bf16[8,8,512]{2,1,0:T(8,128)(2,1)S(1)}, u32[]{:S(2)}, u32[]{:S(2)}) collective-permute-start(bf16[8,8,512]{2,1,0:T(8,128)(2,1)S(1)} %get-tuple-element.27), channel_id=1, source_target_pairs={{0,64},{1,65},{2,66},{3,67},{4,68},{5,69},{6,70},{7,71},{8,72},{9,... | collective-permute-start | bytes 196616 | tf_op jit(solution)/shard_map/ppermute | solution.py:37
  40.0 6.7 %collective-permute-start.9 = (bf16[8,8,512]{2,1,0:T(8,128)(2,1)S(1)}, bf16[8,8,512]{2,1,0:T(8,128)(2,1)S(1)}, u32[]{:S(2)}, u32[]{:S(2)}) collective-permute-start(bf16[8,8,512]{2,1,0:T(8,128)(2,1)S(1)} %get-tuple-element.28), channel_id=1, source_target_pairs={{0,224},{1,225},{2,226},{3,227},{4,228},{5,229},{6,230},{7,231},{8... | collective-permute-start | bytes 196616 | tf_op jit(solution)/shard_map/ppermute | solution.py:37
  42.7 5.1 %collective-permute-start.10 = (bf16[8,8,512]{2,1,0:T(8,128)(2,1)S(1)}, bf16[8,8,512]{2,1,0:T(8,128)(2,1)S(1)}, u32[]{:S(2)}, u32[]{:S(2)}) collective-permute-start(bf16[8,8,512]{2,1,0:T(8,128)(2,1)S(1)} %get-tuple-element.29), channel_id=1, source_target_pairs={{0,32},{1,33},{2,34},{3,35},{4,36},{5,37},{6,38},{7,39},{8,40},{9,... | collective-permute-start | bytes 196616 | tf_op jit(solution)/shard_map/ppermute | solution.py:37
  50.8 6.0 %collective-permute-start.15 = (bf16[32,4096]{1,0:T(8,128)(2,1)S(1)}, bf16[32,4096]{1,0:T(8,128)(2,1)S(1)}, u32[]{:S(2)}, u32[]{:S(2)}) collective-permute-start(bf16[32,4096]{1,0:T(8,128)(2,1)S(1)} %get-tuple-element.34), channel_id=1, source_target_pairs={{0,1},{1,0},{2,3},{3,2},{4,5},{5,4},{6,7},{7,6},{8,9},{9,8},{10,11... | collective-permute-start | bytes 786440 | tf_op jit(solution)/shard_map/ppermute | solution.py:37
  56.9 5.8 %collective-permute-start.16 = (bf16[8,4096]{1,0:T(8,128)(2,1)S(1)}, bf16[8,4096]{1,0:T(8,128)(2,1)S(1)}, u32[]{:S(2)}, u32[]{:S(2)}) collective-permute-start(bf16[8,4096]{1,0:T(8,128)(2,1)S(1)} %get-tuple-element.37), channel_id=1, source_target_pairs={{0,4},{1,5},{2,6},{3,7},{4,0},{5,1},{6,2},{7,3},{8,12},{9,13},{10,... | collective-permute-start | bytes 196616 | tf_op jit(solution)/shard_map/ppermute | solution.py:37
  60.6 3.1 %collective-permute-start.18 = (bf16[8,4096]{1,0:T(8,128)(2,1)S(1)}, bf16[8,4096]{1,0:T(8,128)(2,1)S(1)}, u32[]{:S(2)}, u32[]{:S(2)}) collective-permute-start(bf16[8,4096]{1,0:T(8,128)(2,1)S(1)} %get-tuple-element.38), channel_id=1, source_target_pairs={{0,6},{1,7},{2,0},{3,1},{4,2},{5,3},{6,4},{7,5},{8,14},{9,15},{10,... | collective-permute-start | bytes 196616 | tf_op jit(solution)/shard_map/ppermute | solution.py:37
  61.3 4.3 %collective-permute-start.17 = (bf16[8,4096]{1,0:T(8,128)(2,1)S(1)}, bf16[8,4096]{1,0:T(8,128)(2,1)S(1)}, u32[]{:S(2)}, u32[]{:S(2)}) collective-permute-start(bf16[8,4096]{1,0:T(8,128)(2,1)S(1)} %get-tuple-element.39), channel_id=1, source_target_pairs={{0,2},{1,3},{2,4},{3,5},{4,6},{5,7},{6,0},{7,1},{8,10},{9,11},{10,... | collective-permute-start | bytes 196616 | tf_op jit(solution)/shard_map/ppermute | solution.py:37
  (2 other events, 1.5 us)

commit v2 on v1

v2 whole, which is shorter than its diff:
```python
import jax
import jax.numpy as jnp
from jax import lax
from jax.experimental import pallas as pl
from jax.experimental.pallas import tpu as pltpu
from jax.sharding import PartitionSpec as P

Z, Y, X, C = 8, 4, 4, 2
PIECES, BLK, RANK, W, S = 8, 8, 64, 512, 4096
AXES = ("rows", "rhs")
NT = (((1,), (1,)), ((), ()))
NN = (((1,), (0,)), ((), ()))
TILE = 512
VMEM, SMEM = pl.BlockSpec(memory_space=pltpu.VMEM), pl.BlockSpec(memory_space=pltpu.SMEM)
TURNS = (0, 4)
SENDS = ((0, (0, 1)), (1, (0, 1)), (-1, (0, 1)), (2, (0,)), (-2, (0,)))
TABLE = 16
LONG = pl.CostEstimate(flops=20 << 30, bytes_accessed=1 << 20, transcendentals=0)
LIMIT = pltpu.CompilerParams(vmem_limit_bytes=8 << 20)


def bf16(*shape):
    return jax.ShapeDtypeStruct(shape, jnp.bfloat16)


def f32(*shape):
    return jax.ShapeDtypeStruct(shape, jnp.float32)


def pairs(target):
    place = lambda z, y, x, c: ((z * Y + y) * X + x) * C + c
    return [
        (place(z, y, x, c), place(*target(z, y, x, c)))
        for z in range(Z) for y in range(Y) for x in range(X) for c in range(C)
    ]


def move(part, target):
    return lax.ppermute(part, AXES, pairs(target))


def across_x(part, j):
    return move(part, lambda z, y, x, c: (z, y, x ^ j, c))


def along_y(part, m):
    return part if m == 0 else move(part, lambda z, y, x, c: (z, (y + m) % Y, x, c))


def along_z(part, m):
    return part if m == 0 else move(part, lambda z, y, x, c: ((z + m) % Z, y, x, c))


def other_core(part):
    return move(part, lambda z, y, x, c: (z, y, x, 1 - c))


def pick_kernel(*refs):
    held_refs, asked_ref, out_refs = refs[:Y], refs[Y], refs[Y + 1:-3]
    held_ref, table_ref, sem = refs[-3:]
    copy = pltpu.make_async_copy(asked_ref.at[:, 0], table_ref, sem)
    copy.start()
    row = lax.axis_index("rows")
    y, z = row & 3, row >> 2
    for m in range(Y):
        held_ref[m] = held_refs[m][...]
    copy.wait()
    for (way, parts), out_ref in zip(SENDS, out_refs):
        for b in range(BLK):
            piece = table_ref[(z + way) & 7, b]
            source = (y - (piece >> 3)) & 3
            cols = pl.ds(pl.multiple_of((piece & 7) * W, W), W)
            for n, part in enumerate(parts):
                out_ref[n, b] = held_ref[source, part, :, cols]


def pick(held, asked):
    return pl.pallas_call(
        pick_kernel,
        out_shape=[bf16(len(parts), BLK, 8, W) for _, parts in SENDS],
        in_specs=[VMEM] * Y + [pl.BlockSpec(memory_space=pl.ANY)],
        out_specs=[VMEM] * len(SENDS),
        scratch_shapes=[
            pltpu.VMEM((Y, len(TURNS), 8, PIECES * W), jnp.bfloat16),
            pltpu.SMEM((Z, 128), jnp.int32),
            pltpu.SemaphoreType.DMA,
        ],
        compiler_params=LIMIT,
        cost_estimate=LONG,
        name="pick",
    )(*held, asked)


def halves_kernel(cols_ref, x_ref, table_ref, mine_ref, yours_ref):
    table_ref[...] = jnp.zeros_like(table_ref)
    table_ref[:, :1, :BLK] = jnp.broadcast_to(cols_ref[...], (Z, 1, BLK))
    k = lax.axis_index("rhs")
    x, core = k >> 1, k & 1
    for j in range(X):
        for c, ref in ((core, mine_ref), (1 - core, yours_ref)):
            start = pl.multiple_of(((x ^ j) * 2 + c) * W, W)
            ref[j] = x_ref[:, pl.ds(start, W)]


def halves(far_cols, x_t):
    return pl.pallas_call(
        halves_kernel,
        out_shape=[jax.ShapeDtypeStruct((Z, TABLE, 128), jnp.int32)] + [bf16(X, 8, W)] * 2,
        in_specs=[VMEM] * 2,
        out_specs=[VMEM] * 3,
        compiler_params=LIMIT,
        cost_estimate=LONG,
        name="halves",
    )(far_cols, x_t)


def own_piece(mine, yours):
    parts = jnp.stack([mine, other_core(yours)], 1)
    far = across_x(parts[2:], 2)
    near = across_x(jnp.stack([parts[1], far[1]]), 1)
    return [parts[0], near[0], far[0], near[1]]


def near_kernel(*refs):
    x_refs, (near_ref, out_ref) = refs[:-2], refs[-2:]
    x = jnp.concatenate([r[c].astype(jnp.float32) for c in range(C) for r in x_refs], 0).astype(jnp.bfloat16)
    for t in range(0, S, TILE):
        out_ref[:, t:t + TILE] = lax.dot_general(
            x, near_ref[t:t + TILE, :], NT, preferred_element_type=jnp.float32
        )


def near_product(own, near):
    return pl.pallas_call(
        near_kernel,
        out_shape=f32(64, S),
        in_specs=[VMEM] * (X + 1),
        out_specs=VMEM,
        compiler_params=LIMIT,
        cost_estimate=pl.CostEstimate(flops=2 * 64 * W * S, bytes_accessed=5 << 20, transcendentals=0),
        name="near",
    )(*own, near)


def product_kernel(cls_ref, *refs):
    got_refs, (v_ref, near_ref, u_ref, keep_ref, send_ref, z_buf) = refs[:len(SENDS)], refs[len(SENDS):]
    k, depth = lax.axis_index("rhs"), lax.axis_index("rows") >> 2
    x, core = k >> 1, k & 1
    got = {
        (-way - TURNS[part]) & 7: (ref, n)
        for ref, (way, parts) in zip(got_refs, SENDS) for n, part in enumerate(parts)
    }
    ranks = lax.broadcasted_iota(jnp.int32, (64, RANK), 1)
    halves = []
    for b in range(BLK):
        block = jnp.concatenate([got[d][0][got[d][1], b].astype(jnp.float32) for d in range(Z)], 0).astype(jnp.bfloat16)
        z = lax.dot_general(block, v_ref[b], NT, preferred_element_type=jnp.float32)
        rank = jnp.where(cls_ref[b] == 0, RANK // 4, jnp.where(cls_ref[b] == 1, RANK // 2, RANK))
        halves.append(jnp.where(ranks < rank, z, 0.0))
    for b in range(0, BLK, 2):
        z_buf[b // 2] = jnp.concatenate(halves[b:b + 2], 1).reshape(8, 8, 2 * RANK)
    order = [(x ^ j) * 2 + core for j in range(X)] + [(x ^ j) * 2 + 1 - core for j in range(X)]
    zmask = jnp.concatenate(
        [jnp.concatenate([z_buf[j, (place - depth) & 7] for place in order], 0) for j in range(BLK // 2)], 1
    ).astype(jnp.bfloat16)
    for t in range(0, S, TILE):
        cols = slice(t, t + TILE)
        y = near_ref[:, cols] + lax.dot_general(zmask, u_ref[:, cols], NN, preferred_element_type=jnp.float32)
        keep_ref[:, cols] = y[:32]
        send_ref[:, cols] = y[32:].astype(jnp.bfloat16)


def product(classes, got, v, near, u):
    return pl.pallas_call(
        product_kernel,
        out_shape=(f32(32, S), bf16(32, S)),
        in_specs=[SMEM] + [VMEM] * (len(SENDS) + 3),
        out_specs=(VMEM, VMEM),
        scratch_shapes=[pltpu.VMEM((BLK // 2, 8, 8, 2 * RANK), jnp.float32)],
        compiler_params=LIMIT,
        cost_estimate=pl.CostEstimate(flops=4 * 64 * W * S, bytes_accessed=10 << 20, transcendentals=0),
        name="product",
    )(classes, *got, v, near, u)


def on_device(x_t, far_v, far_u, far_cols, rank_class, near_block):
    both = jnp.stack(
        [move(x_t, lambda z, y, x, c: ((2 * x + c + turn) % Z, y, z // 2, z % 2)) for turn in TURNS]
    )
    asked, kept, given = halves(far_cols, x_t)
    lines = [[z * Y + y for z in range(Z)] for y in range(Y)]
    asked = lax.all_to_all(asked, "rows", 0, 0, axis_index_groups=lines, tiled=True)
    sent = pick([along_y(both, m) for m in range(Y)], asked)
    own = own_piece(kept, given)
    got = [along_z(part, way) for part, (way, _) in zip(sent, SENDS)]
    near = near_product(own, near_block)
    keep, send = product(
        rank_class.reshape(BLK), got, far_v.reshape(BLK, RANK, W), near, far_u.reshape(BLK * RANK, S)
    )
    both = keep + other_core(send).astype(jnp.float32)
    parts = [across_x(both[8 * j:8 * j + 8].astype(jnp.bfloat16), j) for j in (2, 1, 3)]
    total = both[:8]
    for part in parts:
        total = total + part.astype(jnp.float32)
    return total.astype(jnp.bfloat16)


def solution(mesh):
    in_specs = (
        P("rhs", "rows"),
        P("rows", "rhs", None, None),
        P("rows", "rhs", None, None),
        P("rows", "rhs"),
        P("rows", "rhs"),
        P("rows", "rhs"),
    )
    return jax.shard_map(on_device, mesh=mesh, in_specs=in_specs, out_specs=P("rhs", "rows"), check_vma=False)
```

time: 66.5 us -> 57.8 us (0.87); the launches traced: 66.3 us -> 56.7 us
  starting transfers between devices: 45.6 us -> 36 us
  Pallas kernels: 4.38 us -> 5.27 us
  local copies, waits for them, and re-layouts: 1.54 us -> 0.7 us
    ppermute x19 -> x16, starting transfers between devices: 37.6 us -> 30.8 us  [move(): return lax.ppermute(part, AXES, pairs(target))]
    all_to_all x1, starting transfers between devices: 7.93 us -> 5.18 us  [on_device(): lax.all_to_all(asked, 'rows', 0, 0, axis_index_groups=lines, tiled=True)]
    pallas_call x2 -> x3, Pallas kernels: 1.42 us -> 3.58 us  [the longest x1 1.47 us: halves(): pl.pallas_call(halves_kernel, out_shape=[jax.ShapeDtypeStruct((Z, TABLE,...]
    all_to_all x1, waiting for transfers between devices: 1.77 us -> 0.01 us  [on_device(): lax.all_to_all(asked, 'rows', 0, 0, axis_index_groups=lines, tiled=True)]
    ppermute x19 -> x16, waiting for transfers between devices: 12.2 us -> 13.9 us  [move(): return lax.ppermute(part, AXES, pairs(target))]
    pallas_call x1, Pallas kernels: 2.96 us -> 1.69 us  [product(): pl.pallas_call(product_kernel, out_shape=(f32(32, S), bf16(32, S)), in_sp...]
    unnamed x12 -> x10, local copies, waits for them, and re-layouts: 1.52 us -> 0.68 us
  transfers between devices with their start and end apart: 20 -> 17, of which waited for: 11 -> 7; matrix products, arithmetic and copies ran while one was open for 0% -> 0% of each run, Pallas kernels for 2% -> 4%
where the time goes in v2:
time: 57.8 us; the launch traced here: 56.7 us
  starting transfers between devices  36 us (62%)
  waiting for transfers between devices  13.9 us (24%)
  Pallas kernels  5.27 us (9%)
  other arithmetic  0.75 us (1%)
  local copies, waits for them, and re-layouts  0.7 us (1%)
    ppermute x16, starting transfers between devices, move(): return lax.ppermute(part, AXES, pairs(target))  30.8 us
    ppermute x16, waiting for transfers between devices, move(): return lax.ppermute(part, AXES, pairs(target))  13.9 us
    all_to_all x1, starting transfers between devices, on_device(): lax.all_to_all(asked, 'rows', 0, 0, axis_index_groups=lines, tiled=True)  5.18 us
    pallas_call x1, Pallas kernels, product(): pl.pallas_call(product_kernel, out_shape=(f32(32, S), bf16(32, S)), in_sp...  1.69 us
    pallas_call x1, Pallas kernels, halves(): pl.pallas_call(halves_kernel, out_shape=[jax.ShapeDtypeStruct((Z, TABLE,...  1.47 us
    pallas_call x1, Pallas kernels, near_product(): pl.pallas_call(near_kernel, out_shape=f32(64, S), in_specs=[VMEM] * (X +...  1.37 us
  transfers between devices with their start and end apart: 17, of which 7 were waited for; matrix products, arithmetic and copies ran while one was open for 0% of the time, Pallas kernels for 4%

profile of v2, /device:TPU:1, one launch (start us, length us, event | category | flops | bytes accessed | tf_op | source)
XLA Modules:
  0.0 56.7 jit_solution(6898590890900984431)
XLA Ops:
  0.7 1.5 %halves.1 = (s32[8,16,128]{2,1,0:T(8,128)}, bf16[4,8,512]{2,1,0:T(8,128)(2,1)S(1)}, bf16[4,8,512]{2,1,0:T(8,128)(2,1)S(1)}) custom-call(s32[1,8]{1,0:T(1,128)S(1)} %copy-done.4, bf16[8,4096]{1,0:T(8,128)(2,1)} %x_ref.1), custom_call_target="tpu_custom_call" | custom-call | flops 21474836480 | bytes 1048576 | tf_op jit(solution)/shard_map/halves/pallas_call | solution.py:106
  2.1 3.2 %collective-permute-start.9 = (bf16[4,8,512]{2,1,0:T(8,128)(2,1)S(1)}, bf16[4,8,512]{2,1,0:T(8,128)(2,1)S(1)}, u32[]{:S(2)}, u32[]{:S(2)}) collective-permute-start(bf16[4,8,512]{2,1,0:T(8,128)(2,1)S(1)} %get-tuple-element.22), channel_id=1, source_target_pairs={{0,1},{1,0},{2,3},{3,2},{4,5},{5,4},{6,7},{7,6},{8,9},{9,8},{10,11... | collective-permute-start | bytes 98312 | tf_op jit(solution)/shard_map/ppermute | solution.py:39
  5.4 1.9 %collective-permute-start = (bf16[8,4096]{1,0:T(8,128)(2,1)}, bf16[8,4096]{1,0:T(8,128)(2,1)S(1)}, u32[]{:S(2)}, u32[]{:S(2)}) collective-permute-start(bf16[8,4096]{1,0:T(8,128)(2,1)} %x_ref.1), channel_id=1, source_target_pairs={{0,0},{1,32},{2,64},{3,96},{4,128},{5,160},{6,192},{7,224},{8,8},{... | collective-permute-start | bytes 196616 | tf_op jit(solution)/shard_map/ppermute | solution.py:39
  7.3 5.5 %collective-permute-start.1 = (bf16[8,4096]{1,0:T(8,128)(2,1)}, bf16[8,4096]{1,0:T(8,128)(2,1)S(1)}, u32[]{:S(2)}, u32[]{:S(2)}) collective-permute-start(bf16[8,4096]{1,0:T(8,128)(2,1)} %x_ref.1), channel_id=1, source_target_pairs={{0,128},{1,160},{2,192},{3,224},{4,0},{5,32},{6,64},{7,96},{8,136}... | collective-permute-start | bytes 196616 | tf_op jit(solution)/shard_map/ppermute | solution.py:39
  12.8 5.2 %all-to-all-start = ((s32[8,16,128]{2,1,0:T(8,128)}), s32[8,16,128]{2,1,0:T(8,128)S(1)}, u32[]{:S(2)}, u32[]{:S(2)}) async-start(s32[8,16,128]{2,1,0:T(8,128)} %get-tuple-element.15), calls=%async_computation | async-start | bytes 131072 | tf_op jit(solution)/shard_map/all_to_all | solution.py:192
  18.0 3.5 %collective-permute-start.10 = (bf16[2,2,8,512]{3,2,1,0:T(8,128)(2,1)S(1)}, bf16[2,2,8,512]{3,2,1,0:T(8,128)(2,1)S(1)}, u32[]{:S(2)}, u32[]{:S(2)}) collective-permute-start(bf16[2,2,8,512]{3,2,1,0:T(8,128)(2,1)S(1)} %pad_maximum_fusion.1), channel_id=1, source_target_pairs={{0,4},{1,5},{2,6},{3,7},{4,0},{5,1},{6,2},{7,3},{8,12},{9,13},{10,... | collective-permute-start | bytes 98312 | tf_op jit(solution)/shard_map/ppermute | solution.py:39
  21.6 2.8 %collective-permute-start.4 = (bf16[2,8,4096]{2,1,0:T(8,128)(2,1)S(1)}, bf16[2,8,4096]{2,1,0:T(8,128)(2,1)S(1)}, u32[]{:S(2)}, u32[]{:S(2)}) collective-permute-start(bf16[2,8,4096]{2,1,0:T(8,128)(2,1)S(1)} %pad_maximum_fusion.refs_0_), channel_id=1, source_target_pairs={{0,24},{1,25},{2,26},{3,27},{4,28},{5,29},{6,30},{7,31},{8,0},{9,1... | collective-permute-start | bytes 393224 | tf_op jit(solution)/shard_map/ppermute | solution.py:39
  24.7 0.7 %collective-permute-start.2 = (bf16[2,8,4096]{2,1,0:T(8,128)(2,1)S(1)}, bf16[2,8,4096]{2,1,0:T(8,128)(2,1)S(1)}, u32[]{:S(2)}, u32[]{:S(2)}) collective-permute-start(bf16[2,8,4096]{2,1,0:T(8,128)(2,1)S(1)} %pad_maximum_fusion.refs_0_), channel_id=1, source_target_pairs={{0,8},{1,9},{2,10},{3,11},{4,12},{5,13},{6,14},{7,15},{8,16},{9,17... | collective-permute-start | bytes 393224 | tf_op jit(solution)/shard_map/ppermute | solution.py:39
  25.8 0.9 %collective-permute-done.4.refs_3_ = bf16[2,8,4096]{2,1,0:T(8,128)(2,1)S(1)} collective-permute-done((bf16[2,8,4096]{2,1,0:T(8,128)(2,1)S(1)}, bf16[2,8,4096]{2,1,0:T(8,128)(2,1)S(1)}, u32[]{:S(2)}, u32[]{:S(2)}) %collective-permute-start.4) | collective-permute-done | bytes 131104 | tf_op jit(solution)/shard_map/ppermute | solution.py:39
  26.8 3.0 %collective-permute-done.3.refs_2_ = bf16[2,8,4096]{2,1,0:T(8,128)(2,1)S(1)} collective-permute-done((bf16[2,8,4096]{2,1,0:T(8,128)(2,1)S(1)}, bf16[2,8,4096]{2,1,0:T(8,128)(2,1)S(1)}, u32[]{:S(2)}, u32[]{:S(2)}) %collective-permute-start.3) | collective-permute-done | bytes 131104 | tf_op jit(solution)/shard_map/ppermute | solution.py:39
  29.8 3.2 %collective-permute-done.2.refs_1_ = bf16[2,8,4096]{2,1,0:T(8,128)(2,1)S(1)} collective-permute-done((bf16[2,8,4096]{2,1,0:T(8,128)(2,1)S(1)}, bf16[2,8,4096]{2,1,0:T(8,128)(2,1)S(1)}, u32[]{:S(2)}, u32[]{:S(2)}) %collective-permute-start.2) | collective-permute-done | bytes 131104 | tf_op jit(solution)/shard_map/ppermute | solution.py:39
  33.0 0.7 %pick.1 = (bf16[2,8,8,512]{3,2,1,0:T(8,128)(2,1)S(1)}, bf16[2,8,8,512]{3,2,1,0:T(8,128)(2,1)S(1)}, bf16[2,8,8,512]{3,2,1,0:T(8,128)(2,1)S(1)}, bf16[1,8,8,512]{3...) custom-call(bf16[2,8,4096]{2,1,0:T(8,128)(2,1)S(1)} %pad_maximum_fusion.refs_0_, ...), custom_call_target="tpu_custom_call" | custom-call | flops 21474836480 | bytes 1048576 | tf_op jit(solution)/shard_map/pick/pallas_call | solution.py:78
  33.8 0.9 %collective-permute-start.7 = (bf16[1,8,8,512]{3,2,1,0:T(8,128)(2,1)S(1)}, bf16[1,8,8,512]{3,2,1,0:T(8,128)(2,1)S(1)}, u32[]{:S(2)}, u32[]{:S(2)}) collective-permute-start(bf16[1,8,8,512]{3,2,1,0:T(8,128)(2,1)S(1)} %get-tuple-element.19), channel_id=1, source_target_pairs={{0,64},{1,65},{2,66},{3,67},{4,68},{5,69},{6,70},{7,71},{8,72},{9,... | collective-permute-start | bytes 196616 | tf_op jit(solution)/shard_map/ppermute | solution.py:39
  34.8 2.7 %collective-permute-start.8 = (bf16[1,8,8,512]{3,2,1,0:T(8,128)(2,1)S(1)}, bf16[1,8,8,512]{3,2,1,0:T(8,128)(2,1)S(1)}, u32[]{:S(2)}, u32[]{:S(2)}) collective-permute-start(bf16[1,8,8,512]{3,2,1,0:T(8,128)(2,1)S(1)} %get-tuple-element.20), channel_id=1, source_target_pairs={{0,192},{1,193},{2,194},{3,195},{4,196},{5,197},{6,198},{7,199},{8... | collective-permute-start | bytes 196616 | tf_op jit(solution)/shard_map/ppermute | solution.py:39
  37.5 2.7 %collective-permute-start.6 = (bf16[2,8,8,512]{3,2,1,0:T(8,128)(2,1)S(1)}, bf16[2,8,8,512]{3,2,1,0:T(8,128)(2,1)S(1)}, u32[]{:S(2)}, u32[]{:S(2)}) collective-permute-start(bf16[2,8,8,512]{3,2,1,0:T(8,128)(2,1)S(1)} %get-tuple-element.18), channel_id=1, source_target_pairs={{0,224},{1,225},{2,226},{3,227},{4,228},{5,229},{6,230},{7,231},{8... | collective-permute-start | bytes 393224 | tf_op jit(solution)/shard_map/ppermute | solution.py:39
  40.2 1.4 %near.1.refs_6_ = f32[64,4096]{1,0:T(8,128)S(1)} custom-call(bf16[2,8,512]{2,1,0:T(8,128)(2,1)S(1)} %maximum_bitcast_fusion.refs_0_, bf16[2,8,512]{2,1,0:T(8,128)(2,1)S(1)} %get-tuple-element.31.refs_1_, bf16[2,8,512]{2,1,0:T(8,128)(2,1)S(1)} %get-tuple-element.32.refs_2_, bf16[2,8,512]{2,1,0:T(8,128)(2,1)S(1)} %get-tuple-element.30.refs_3_, ...), custom_call_target="tpu_custom_call" | custom-call | flops 268435456 | bytes 5242880 | tf_op jit(solution)/shard_map/near/pallas_call | solution.py:134
  41.6 2.0 %collective-permute-done.5.refs_1_ = bf16[2,8,8,512]{3,2,1,0:T(8,128)(2,1)S(1)} collective-permute-done((bf16[2,8,8,512]{3,2,1,0:T(8,128)(2,1)S(1)}, bf16[2,8,8,512]{3,2,1,0:T(8,128)(2,1)S(1)}, u32[]{:S(2)}, u32[]{:S(2)}) %collective-permute-start.5) | collective-permute-done | bytes 131104 | tf_op jit(solution)/shard_map/ppermute | solution.py:39
  43.5 1.7 %product.1 = (f32[32,4096]{1,0:T(8,128)S(1)}, bf16[32,4096]{1,0:T(8,128)(2,1)S(1)}) custom-call(s32[8]{0:T(128)S(1)} %bitcast.20, bf16[2,8,8,512]{3,2,1,0:T(8,128)(2,1)S(1)} %get-tuple-element.16.refs_0_, bf16[2,8,8,512]{3,2,1,0:T(8,128)(2,1)S(1)} %collective-permute-done.5.refs_1_, bf16[2,8,8,512]{3,2,1,0:T(8,128)(2,1)S(1)} %collective-permute-done.6.refs_2_, ...), custom_call_target="tpu_custom_call" | custom-call | flops 536870912 | bytes 10485760 | tf_op jit(solution)/shard_map/product/pallas_call | solution.py:174
  45.2 2.9 %collective-permute-start.12 = (bf16[32,4096]{1,0:T(8,128)(2,1)S(1)}, bf16[32,4096]{1,0:T(8,128)(2,1)S(1)}, u32[]{:S(2)}, u32[]{:S(2)}) collective-permute-start(bf16[32,4096]{1,0:T(8,128)(2,1)S(1)} %get-tuple-element.24), channel_id=1, source_target_pairs={{0,1},{1,0},{2,3},{3,2},{4,5},{5,4},{6,7},{7,6},{8,9},{9,8},{10,11... | collective-permute-start | bytes 786440 | tf_op jit(solution)/shard_map/ppermute | solution.py:39
  48.1 1.2 %collective-permute-done.12 = bf16[32,4096]{1,0:T(8,128)(2,1)S(1)} collective-permute-done((bf16[32,4096]{1,0:T(8,128)(2,1)S(1)}, bf16[32,4096]{1,0:T(8,128)(2,1)S(1)}, u32[]{:S(2)}, u32[]{:S(2)}) %collective-permute-start.12) | collective-permute-done | bytes 262176 | tf_op jit(solution)/shard_map/ppermute | solution.py:39
  49.3 1.1 %collective-permute-start.13 = (bf16[8,4096]{1,0:T(8,128)(2,1)S(1)}, bf16[8,4096]{1,0:T(8,128)(2,1)S(1)}, u32[]{:S(2)}, u32[]{:S(2)}) collective-permute-start(bf16[8,4096]{1,0:T(8,128)(2,1)S(1)} %get-tuple-element.27), channel_id=1, source_target_pairs={{0,4},{1,5},{2,6},{3,7},{4,0},{5,1},{6,2},{7,3},{8,12},{9,13},{10,... | collective-permute-start | bytes 196616 | tf_op jit(solution)/shard_map/ppermute | solution.py:39
  50.4 1.7 %collective-permute-start.15 = (bf16[8,4096]{1,0:T(8,128)(2,1)S(1)}, bf16[8,4096]{1,0:T(8,128)(2,1)S(1)}, u32[]{:S(2)}, u32[]{:S(2)}) collective-permute-start(bf16[8,4096]{1,0:T(8,128)(2,1)S(1)} %get-tuple-element.28), channel_id=1, source_target_pairs={{0,6},{1,7},{2,4},{3,5},{4,2},{5,3},{6,0},{7,1},{8,14},{9,15},{10,... | collective-permute-start | bytes 196616 | tf_op jit(solution)/shard_map/ppermute | solution.py:39
  52.5 1.5 %collective-permute-done.13 = bf16[8,4096]{1,0:T(8,128)(2,1)S(1)} collective-permute-done((bf16[8,4096]{1,0:T(8,128)(2,1)S(1)}, bf16[8,4096]{1,0:T(8,128)(2,1)S(1)}, u32[]{:S(2)}, u32[]{:S(2)}) %collective-permute-start.13) | collective-permute-done | bytes 65568 | tf_op jit(solution)/shard_map/ppermute | solution.py:39
  54.0 2.0 %collective-permute-done.15 = bf16[8,4096]{1,0:T(8,128)(2,1)S(1)} collective-permute-done((bf16[8,4096]{1,0:T(8,128)(2,1)S(1)}, bf16[8,4096]{1,0:T(8,128)(2,1)S(1)}, u32[]{:S(2)}, u32[]{:S(2)}) %collective-permute-start.15) | collective-permute-done | bytes 65568 | tf_op jit(solution)/shard_map/ppermute | solution.py:39
  (33 shorter events, 2.6 us)
Async XLA Ops:
  0.0 0.7 %copy-start.4 = (s32[1,8]{1,0:T(1,128)S(1)}, s32[1,8]{1,0:T(1,128)}, u32[]{:S(2)}) copy-start(s32[1,8]{1,0:T(1,128)} %cols_ref.1) | copy-start | bytes 100
  2.1 15.9 %collective-permute-start.9 = (bf16[4,8,512]{2,1,0:T(8,128)(2,1)S(1)}, bf16[4,8,512]{2,1,0:T(8,128)(2,1)S(1)}, u32[]{:S(2)}, u32[]{:S(2)}) collective-permute-start(bf16[4,8,512]{2,1,0:T(8,128)(2,1)S(1)} %get-tuple-element.22), channel_id=1, source_target_pairs={{0,1},{1,0},{2,3},{3,2},{4,5},{5,4},{6,7},{7,6},{8,9},{9,8},{10,11... | collective-permute-start | bytes 98312 | tf_op jit(solution)/shard_map/ppermute | solution.py:39
  5.4 16.2 %collective-permute-start = (bf16[8,4096]{1,0:T(8,128)(2,1)}, bf16[8,4096]{1,0:T(8,128)(2,1)S(1)}, u32[]{:S(2)}, u32[]{:S(2)}) collective-permute-start(bf16[8,4096]{1,0:T(8,128)(2,1)} %x_ref.1), channel_id=1, source_target_pairs={{0,0},{1,32},{2,64},{3,96},{4,128},{5,160},{6,192},{7,224},{8,8},{... | collective-permute-start | bytes 196616 | tf_op jit(solution)/shard_map/ppermute | solution.py:39
  7.3 14.2 %collective-permute-start.1 = (bf16[8,4096]{1,0:T(8,128)(2,1)}, bf16[8,4096]{1,0:T(8,128)(2,1)S(1)}, u32[]{:S(2)}, u32[]{:S(2)}) collective-permute-start(bf16[8,4096]{1,0:T(8,128)(2,1)} %x_ref.1), channel_id=1, source_target_pairs={{0,128},{1,160},{2,192},{3,224},{4,0},{5,32},{6,64},{7,96},{8,136}... | collective-permute-start | bytes 196616 | tf_op jit(solution)/shard_map/ppermute | solution.py:39
  12.8 13.0 %all-to-all-start = ((s32[8,16,128]{2,1,0:T(8,128)}), s32[8,16,128]{2,1,0:T(8,128)S(1)}, u32[]{:S(2)}, u32[]{:S(2)}) async-start(s32[8,16,128]{2,1,0:T(8,128)} %get-tuple-element.15), calls=%async_computation | async-start | bytes 131072 | tf_op jit(solution)/shard_map/all_to_all | solution.py:192
  18.0 7.4 %collective-permute-start.10 = (bf16[2,2,8,512]{3,2,1,0:T(8,128)(2,1)S(1)}, bf16[2,2,8,512]{3,2,1,0:T(8,128)(2,1)S(1)}, u32[]{:S(2)}, u32[]{:S(2)}) collective-permute-start(bf16[2,2,8,512]{3,2,1,0:T(8,128)(2,1)S(1)} %pad_maximum_fusion.1), channel_id=1, source_target_pairs={{0,4},{1,5},{2,6},{3,7},{4,0},{5,1},{6,2},{7,3},{8,12},{9,13},{10,... | collective-permute-start | bytes 98312 | tf_op jit(solution)/shard_map/ppermute | solution.py:39
  21.6 5.2 %collective-permute-start.4 = (bf16[2,8,4096]{2,1,0:T(8,128)(2,1)S(1)}, bf16[2,8,4096]{2,1,0:T(8,128)(2,1)S(1)}, u32[]{:S(2)}, u32[]{:S(2)}) collective-permute-start(bf16[2,8,4096]{2,1,0:T(8,128)(2,1)S(1)} %pad_maximum_fusion.refs_0_), channel_id=1, source_target_pairs={{0,24},{1,25},{2,26},{3,27},{4,28},{5,29},{6,30},{7,31},{8,0},{9,1... | collective-permute-start | bytes 393224 | tf_op jit(solution)/shard_map/ppermute | solution.py:39
  24.4 5.4 %collective-permute-start.3 = (bf16[2,8,4096]{2,1,0:T(8,128)(2,1)S(1)}, bf16[2,8,4096]{2,1,0:T(8,128)(2,1)S(1)}, u32[]{:S(2)}, u32[]{:S(2)}) collective-permute-start(bf16[2,8,4096]{2,1,0:T(8,128)(2,1)S(1)} %pad_maximum_fusion.refs_0_), channel_id=1, source_target_pairs={{0,16},{1,17},{2,18},{3,19},{4,20},{5,21},{6,22},{7,23},{8,24},{9,... | collective-permute-start | bytes 393224 | tf_op jit(solution)/shard_map/ppermute | solution.py:39
  24.7 8.3 %collective-permute-start.2 = (bf16[2,8,4096]{2,1,0:T(8,128)(2,1)S(1)}, bf16[2,8,4096]{2,1,0:T(8,128)(2,1)S(1)}, u32[]{:S(2)}, u32[]{:S(2)}) collective-permute-start(bf16[2,8,4096]{2,1,0:T(8,128)(2,1)S(1)} %pad_maximum_fusion.refs_0_), channel_id=1, source_target_pairs={{0,8},{1,9},{2,10},{3,11},{4,12},{5,13},{6,14},{7,15},{8,16},{9,17... | collective-permute-start | bytes 393224 | tf_op jit(solution)/shard_map/ppermute | solution.py:39
  25.4 14.7 %collective-permute-start.11 = (bf16[2,2,8,512]{3,2,1,0:T(8,128)(2,1)S(1)}, bf16[2,2,8,512]{3,2,1,0:T(8,128)(2,1)S(1)}, u32[]{:S(2)}, u32[]{:S(2)}) collective-permute-start(bf16[2,2,8,512]{3,2,1,0:T(8,128)(2,1)S(1)} %fusion.6), channel_id=1, source_target_pairs={{0,2},{1,3},{2,0},{3,1},{4,6},{5,7},{6,4},{7,5},{8,10},{9,11},{10,... | collective-permute-start | bytes 98312 | tf_op jit(solution)/shard_map/ppermute | solution.py:39
  25.8 14.3 %copy-start.1 = (bf16[4096,512]{1,0:T(8,128)(2,1)S(1)}, bf16[4096,512]{1,0:T(8,128)(2,1)}, u32[]{:S(2)}) copy-start(bf16[4096,512]{1,0:T(8,128)(2,1)} %refs_4_.1) | copy-start | bytes 12582916
  33.8 9.7 %copy-start = (bf16[1,8,64,4096]{3,2,1,0:T(8,128)(2,1)S(1)}, bf16[1,8,64,4096]{3,2,1,0:T(8,128)(2,1)}, u32[]{:S(2)}) copy-start(bf16[1,8,64,4096]{3,2,1,0:T(8,128)(2,1)} %param.8) | copy-start | bytes 12582916
  33.8 9.7 %copy-start.2 = (bf16[1,8,64,512]{3,2,1,0:T(8,128)(2,1)S(1)}, bf16[1,8,64,512]{3,2,1,0:T(8,128)(2,1)}, u32[]{:S(2)}) copy-start(bf16[1,8,64,512]{3,2,1,0:T(8,128)(2,1)} %param.7) | copy-start | bytes 1572868
  33.8 9.7 %copy-start.3 = (s32[1,8]{1,0:T(1,128)S(1)}, s32[1,8]{1,0:T(1,128)}, u32[]{:S(2)}) copy-start(s32[1,8]{1,0:T(1,128)} %param.10) | copy-start | bytes 100
  33.8 7.7 %collective-permute-start.7 = (bf16[1,8,8,512]{3,2,1,0:T(8,128)(2,1)S(1)}, bf16[1,8,8,512]{3,2,1,0:T(8,128)(2,1)S(1)}, u32[]{:S(2)}, u32[]{:S(2)}) collective-permute-start(bf16[1,8,8,512]{3,2,1,0:T(8,128)(2,1)S(1)} %get-tuple-element.19), channel_id=1, source_target_pairs={{0,64},{1,65},{2,66},{3,67},{4,68},{5,69},{6,70},{7,71},{8,72},{9,... | collective-permute-start | bytes 196616 | tf_op jit(solution)/shard_map/ppermute | solution.py:39
  34.8 6.8 %collective-permute-start.8 = (bf16[1,8,8,512]{3,2,1,0:T(8,128)(2,1)S(1)}, bf16[1,8,8,512]{3,2,1,0:T(8,128)(2,1)S(1)}, u32[]{:S(2)}, u32[]{:S(2)}) collective-permute-start(bf16[1,8,8,512]{3,2,1,0:T(8,128)(2,1)S(1)} %get-tuple-element.20), channel_id=1, source_target_pairs={{0,192},{1,193},{2,194},{3,195},{4,196},{5,197},{6,198},{7,199},{8... | collective-permute-start | bytes 196616 | tf_op jit(solution)/shard_map/ppermute | solution.py:39
  37.5 6.0 %collective-permute-start.5 = (bf16[2,8,8,512]{3,2,1,0:T(8,128)(2,1)S(1)}, bf16[2,8,8,512]{3,2,1,0:T(8,128)(2,1)S(1)}, u32[]{:S(2)}, u32[]{:S(2)}) collective-permute-start(bf16[2,8,8,512]{3,2,1,0:T(8,128)(2,1)S(1)} %get-tuple-element.17), channel_id=1, source_target_pairs={{0,32},{1,33},{2,34},{3,35},{4,36},{5,37},{6,38},{7,39},{8,40},{9,... | collective-permute-start | bytes 393224 | tf_op jit(solution)/shard_map/ppermute | solution.py:39
  37.5 6.0 %collective-permute-start.6 = (bf16[2,8,8,512]{3,2,1,0:T(8,128)(2,1)S(1)}, bf16[2,8,8,512]{3,2,1,0:T(8,128)(2,1)S(1)}, u32[]{:S(2)}, u32[]{:S(2)}) collective-permute-start(bf16[2,8,8,512]{3,2,1,0:T(8,128)(2,1)S(1)} %get-tuple-element.18), channel_id=1, source_target_pairs={{0,224},{1,225},{2,226},{3,227},{4,228},{5,229},{6,230},{7,231},{8... | collective-permute-start | bytes 393224 | tf_op jit(solution)/shard_map/ppermute | solution.py:39
  45.2 4.0 %collective-permute-start.12 = (bf16[32,4096]{1,0:T(8,128)(2,1)S(1)}, bf16[32,4096]{1,0:T(8,128)(2,1)S(1)}, u32[]{:S(2)}, u32[]{:S(2)}) collective-permute-start(bf16[32,4096]{1,0:T(8,128)(2,1)S(1)} %get-tuple-element.24), channel_id=1, source_target_pairs={{0,1},{1,0},{2,3},{3,2},{4,5},{5,4},{6,7},{7,6},{8,9},{9,8},{10,11... | collective-permute-start | bytes 786440 | tf_op jit(solution)/shard_map/ppermute | solution.py:39
  49.3 4.7 %collective-permute-start.13 = (bf16[8,4096]{1,0:T(8,128)(2,1)S(1)}, bf16[8,4096]{1,0:T(8,128)(2,1)S(1)}, u32[]{:S(2)}, u32[]{:S(2)}) collective-permute-start(bf16[8,4096]{1,0:T(8,128)(2,1)S(1)} %get-tuple-element.27), channel_id=1, source_target_pairs={{0,4},{1,5},{2,6},{3,7},{4,0},{5,1},{6,2},{7,3},{8,12},{9,13},{10,... | collective-permute-start | bytes 196616 | tf_op jit(solution)/shard_map/ppermute | solution.py:39
  50.4 5.6 %collective-permute-start.15 = (bf16[8,4096]{1,0:T(8,128)(2,1)S(1)}, bf16[8,4096]{1,0:T(8,128)(2,1)S(1)}, u32[]{:S(2)}, u32[]{:S(2)}) collective-permute-start(bf16[8,4096]{1,0:T(8,128)(2,1)S(1)} %get-tuple-element.28), channel_id=1, source_target_pairs={{0,6},{1,7},{2,4},{3,5},{4,2},{5,3},{6,0},{7,1},{8,14},{9,15},{10,... | collective-permute-start | bytes 196616 | tf_op jit(solution)/shard_map/ppermute | solution.py:39
  52.1 3.9 %collective-permute-start.14 = (bf16[8,4096]{1,0:T(8,128)(2,1)S(1)}, bf16[8,4096]{1,0:T(8,128)(2,1)S(1)}, u32[]{:S(2)}, u32[]{:S(2)}) collective-permute-start(bf16[8,4096]{1,0:T(8,128)(2,1)S(1)} %get-tuple-element.29), channel_id=1, source_target_pairs={{0,2},{1,3},{2,0},{3,1},{4,6},{5,7},{6,4},{7,5},{8,10},{9,11},{10,... | collective-permute-start | bytes 196616 | tf_op jit(solution)/shard_map/ppermute | solution.py:39

commit v3 on v2

--- a/solution.py
+++ b/solution.py
@@ -13,8 +13,7 @@
 TILE = 512
 VMEM, SMEM = pl.BlockSpec(memory_space=pltpu.VMEM), pl.BlockSpec(memory_space=pltpu.SMEM)
 TURNS = (0, 4)
-SENDS = ((0, (0, 1)), (1, (0, 1)), (-1, (0, 1)), (2, (0,)), (-2, (0,)))
-TABLE = 16
+SENDS = ((0, (0, 1)), (2, (0, 1)), (1, (0, 1)), (-1, (0, 1)))
 LONG = pl.CostEstimate(flops=20 << 30, bytes_accessed=1 << 20, transcendentals=0)
 LIMIT = pltpu.CompilerParams(vmem_limit_bytes=8 << 20)
 
@@ -39,6 +38,18 @@
     return lax.ppermute(part, AXES, pairs(target))
 
 
+def turned(way, core):
+    return way * (1 - 2 * core) if way == 2 else way
+
+
+def send_z(part, way):
+    return move(part, lambda z, y, x, c: ((z + turned(way, c)) % Z, y, x, c))
+
+
+def ask_z(part, way):
+    return move(part, lambda z, y, x, c: ((z - turned(way, c)) % Z, y, x, c))
+
+
 def across_x(part, j):
     return move(part, lambda z, y, x, c: (z, y, x ^ j, c))
 
@@ -47,53 +58,39 @@
     return part if m == 0 else move(part, lambda z, y, x, c: (z, (y + m) % Y, x, c))
 
 
-def along_z(part, m):
-    return part if m == 0 else move(part, lambda z, y, x, c: ((z + m) % Z, y, x, c))
-
-
 def other_core(part):
     return move(part, lambda z, y, x, c: (z, y, x, 1 - c))
 
 
 def pick_kernel(*refs):
-    held_refs, asked_ref, out_refs = refs[:Y], refs[Y], refs[Y + 1:-3]
-    held_ref, table_ref, sem = refs[-3:]
-    copy = pltpu.make_async_copy(asked_ref.at[:, 0], table_ref, sem)
-    copy.start()
-    row = lax.axis_index("rows")
-    y, z = row & 3, row >> 2
+    n = len(SENDS)
+    held_refs, asked_refs, out_refs, held_ref = refs[:Y], refs[Y:Y + n], refs[Y + n:-1], refs[-1]
+    y, core = lax.axis_index("rows") & 3, lax.axis_index("rhs") & 1
     for m in range(Y):
         held_ref[m] = held_refs[m][...]
-    copy.wait()
-    for (way, parts), out_ref in zip(SENDS, out_refs):
+    for (way, parts), asked_ref, out_ref in zip(SENDS, asked_refs, out_refs):
         for b in range(BLK):
-            piece = table_ref[(z + way) & 7, b]
+            piece = asked_ref[0, b]
             source = (y - (piece >> 3)) & 3
             cols = pl.ds(pl.multiple_of((piece & 7) * W, W), W)
             for n, part in enumerate(parts):
-                out_ref[n, b] = held_ref[source, part, :, cols]
+                out_ref[n, b] = held_ref[source, part ^ core if way == 2 else part, :, cols]
 
 
 def pick(held, asked):
     return pl.pallas_call(
         pick_kernel,
         out_shape=[bf16(len(parts), BLK, 8, W) for _, parts in SENDS],
-        in_specs=[VMEM] * Y + [pl.BlockSpec(memory_space=pl.ANY)],
+        in_specs=[VMEM] * Y + [SMEM] * len(SENDS),
         out_specs=[VMEM] * len(SENDS),
-        scratch_shapes=[
-            pltpu.VMEM((Y, len(TURNS), 8, PIECES * W), jnp.bfloat16),
-            pltpu.SMEM((Z, 128), jnp.int32),
-            pltpu.SemaphoreType.DMA,
-        ],
+        scratch_shapes=[pltpu.VMEM((Y, len(TURNS), 8, PIECES * W), jnp.bfloat16)],
         compiler_params=LIMIT,
         cost_estimate=LONG,
         name="pick",
-    )(*held, asked)
-
-
-def halves_kernel(cols_ref, x_ref, table_ref, mine_ref, yours_ref):
-    table_ref[...] = jnp.zeros_like(table_ref)
-    table_ref[:, :1, :BLK] = jnp.broadcast_to(cols_ref[...], (Z, 1, BLK))
+    )(*held, *asked)
+
+
+def halves_kernel(x_ref, mine_ref, yours_ref):
     k = lax.axis_index("rhs")
     x, core = k >> 1, k & 1
     for j in range(X):
@@ -102,16 +99,16 @@
             ref[j] = x_ref[:, pl.ds(start, W)]
 
 
-def halves(far_cols, x_t):
+def halves(x_t):
     return pl.pallas_call(
         halves_kernel,
-        out_shape=[jax.ShapeDtypeStruct((Z, TABLE, 128), jnp.int32)] + [bf16(X, 8, W)] * 2,
-        in_specs=[VMEM] * 2,
-        out_specs=[VMEM] * 3,
+        out_shape=[bf16(X, 8, W)] * 2,
+        in_specs=[VMEM],
+        out_specs=[VMEM] * 2,
         compiler_params=LIMIT,
         cost_estimate=LONG,
         name="halves",
-    )(far_cols, x_t)
+    )(x_t)
 
 
 def own_piece(mine, yours):
@@ -187,12 +184,11 @@
     both = jnp.stack(
         [move(x_t, lambda z, y, x, c: ((2 * x + c + turn) % Z, y, z // 2, z % 2)) for turn in TURNS]
     )
-    asked, kept, given = halves(far_cols, x_t)
-    lines = [[z * Y + y for z in range(Z)] for y in range(Y)]
-    asked = lax.all_to_all(asked, "rows", 0, 0, axis_index_groups=lines, tiled=True)
+    own = own_piece(*halves(x_t))
+    both, asked = lax.optimization_barrier((both, far_cols))
+    asked = [asked if way == 0 else ask_z(asked, way) for way, _ in SENDS]
     sent = pick([along_y(both, m) for m in range(Y)], asked)
-    own = own_piece(kept, given)
-    got = [along_z(part, way) for part, (way, _) in zip(sent, SENDS)]
+    got = [part if way == 0 else send_z(part, way) for part, (way, _) in zip(sent, SENDS)]
     near = near_product(own, near_block)
     keep, send = product(
         rank_class.reshape(BLK), got, far_v.reshape(BLK, RANK, W), near, far_u.reshape(BLK * RANK, S)

time: 57.8 us -> 54.6 us (0.945); the launches traced: 56.7 us -> 54.5 us
  starting transfers between devices: 36 us -> 27.8 us
  waiting for transfers between devices: 13.9 us -> 21.1 us
  Pallas kernels: 5.27 us -> 4.6 us
  local copies, waits for them, and re-layouts: 0.7 us -> 0.05 us
    ppermute x16 -> x18, waiting for transfers between devices: 13.9 us -> 21.1 us  [move(): return lax.ppermute(part, AXES, pairs(target))]
    all_to_all x1 -> x0, starting transfers between devices: 5.18 us -> none  [on_device(): lax.all_to_all(asked, 'rows', 0, 0, axis_index_groups=lines, tiled=True)]
    ppermute x16 -> x18, starting transfers between devices: 30.8 us -> 27.8 us  [move(): return lax.ppermute(part, AXES, pairs(target))]
    unnamed x10, local copies, waits for them, and re-layouts: 0.68 us -> 0.03 us
    pallas_call x1, Pallas kernels: 1.47 us -> 0.86 us  [halves(): pl.pallas_call(halves_kernel, out_shape=[bf16(X, 8, W)] * 2, in_specs=[VM...]
  transfers between devices with their start and end apart: 17 -> 18, of which waited for: 7 -> 9; matrix products, arithmetic and copies ran while one was open for 0% -> 0% of each run, Pallas kernels for 4% -> 4%
where the time goes in v3:
time: 54.6 us; the launch traced here: 54.5 us
  starting transfers between devices  27.8 us (51%)
  waiting for transfers between devices  21.1 us (39%)
  Pallas kernels  4.6 us (8%)
  other arithmetic  0.75 us (1%)
    ppermute x18, starting transfers between devices, move(): return lax.ppermute(part, AXES, pairs(target))  27.8 us
    ppermute x18, waiting for transfers between devices, move(): return lax.ppermute(part, AXES, pairs(target))  21.1 us
    pallas_call x1, Pallas kernels, product(): pl.pallas_call(product_kernel, out_shape=(f32(32, S), bf16(32, S)), in_sp...  1.69 us
    pallas_call x1, Pallas kernels, near_product(): pl.pallas_call(near_kernel, out_shape=f32(64, S), in_specs=[VMEM] * (X +...  1.37 us
  transfers between devices with their start and end apart: 18, of which 9 were waited for; matrix products, arithmetic and copies ran while one was open for 0% of the time, Pallas kernels for 4%

profile of v3, /device:TPU:1, one launch (start us, length us, event | category | flops | bytes accessed | tf_op | source)
XLA Modules:
  0.0 54.5 jit_solution(11025067009963099483)
XLA Ops:
  0.0 0.9 %halves.1 = (bf16[4,8,512]{2,1,0:T(8,128)(2,1)S(1)}, bf16[4,8,512]{2,1,0:T(8,128)(2,1)S(1)}) custom-call(bf16[8,4096]{1,0:T(8,128)(2,1)} %x_ref.1), custom_call_target="tpu_custom_call" | custom-call | flops 21474836480 | bytes 1048576 | tf_op jit(solution)/shard_map/halves/pallas_call | solution.py:103
  0.9 3.2 %collective-permute-start.11 = (bf16[4,8,512]{2,1,0:T(8,128)(2,1)S(1)}, bf16[4,8,512]{2,1,0:T(8,128)(2,1)S(1)}, u32[]{:S(2)}, u32[]{:S(2)}) collective-permute-start(bf16[4,8,512]{2,1,0:T(8,128)(2,1)S(1)} %get-tuple-element.22), channel_id=1, source_target_pairs={{0,1},{1,0},{2,3},{3,2},{4,5},{5,4},{6,7},{7,6},{8,9},{9,8},{10,11... | collective-permute-start | bytes 98312 | tf_op jit(solution)/shard_map/ppermute | solution.py:38
  4.1 1.9 %collective-permute-start = (bf16[8,4096]{1,0:T(8,128)(2,1)}, bf16[8,4096]{1,0:T(8,128)(2,1)S(1)}, u32[]{:S(2)}, u32[]{:S(2)}) collective-permute-start(bf16[8,4096]{1,0:T(8,128)(2,1)} %x_ref.1), channel_id=1, source_target_pairs={{0,0},{1,32},{2,64},{3,96},{4,128},{5,160},{6,192},{7,224},{8,8},{... | collective-permute-start | bytes 196616 | tf_op jit(solution)/shard_map/ppermute | solution.py:38
  6.0 5.5 %collective-permute-start.1 = (bf16[8,4096]{1,0:T(8,128)(2,1)}, bf16[8,4096]{1,0:T(8,128)(2,1)S(1)}, u32[]{:S(2)}, u32[]{:S(2)}) collective-permute-start(bf16[8,4096]{1,0:T(8,128)(2,1)} %x_ref.1), channel_id=1, source_target_pairs={{0,128},{1,160},{2,192},{3,224},{4,0},{5,32},{6,64},{7,96},{8,136}... | collective-permute-start | bytes 196616 | tf_op jit(solution)/shard_map/ppermute | solution.py:38
  11.6 2.0 %collective-permute-start.12 = (bf16[2,2,8,512]{3,2,1,0:T(8,128)(2,1)S(1)}, bf16[2,2,8,512]{3,2,1,0:T(8,128)(2,1)S(1)}, u32[]{:S(2)}, u32[]{:S(2)}) collective-permute-start(bf16[2,2,8,512]{3,2,1,0:T(8,128)(2,1)S(1)} %pad_maximum_fusion.1), channel_id=1, source_target_pairs={{0,4},{1,5},{2,6},{3,7},{4,0},{5,1},{6,2},{7,3},{8,12},{9,13},{10,... | collective-permute-start | bytes 98312 | tf_op jit(solution)/shard_map/ppermute | solution.py:38
  13.5 4.7 %collective-permute-done.1 = bf16[8,4096]{1,0:T(8,128)(2,1)S(1)} collective-permute-done((bf16[8,4096]{1,0:T(8,128)(2,1)}, bf16[8,4096]{1,0:T(8,128)(2,1)S(1)}, u32[]{:S(2)}, u32[]{:S(2)}) %collective-permute-start.1) | collective-permute-done | bytes 65568 | tf_op jit(solution)/shard_map/ppermute | solution.py:38
  18.4 2.7 %collective-permute-start.6 = (s32[1,8]{1,0:T(1,128)S(1)}, s32[1,8]{1,0:T(1,128)S(1)}, u32[]{:S(2)}, u32[]{:S(2)}) collective-permute-start(s32[1,8]{1,0:T(1,128)S(1)} %copy-done.4), channel_id=1, source_target_pairs={{0,224},{1,225},{2,226},{3,227},{4,228},{5,229},{6,230},{7,231},{8... | collective-permute-start | bytes 104 | tf_op jit(solution)/shard_map/ppermute | solution.py:38
  21.0 2.7 %collective-permute-start.4 = (bf16[2,8,4096]{2,1,0:T(8,128)(2,1)S(1)}, bf16[2,8,4096]{2,1,0:T(8,128)(2,1)S(1)}, u32[]{:S(2)}, u32[]{:S(2)}) collective-permute-start(bf16[2,8,4096]{2,1,0:T(8,128)(2,1)S(1)} %pad_maximum_fusion.refs_0_), channel_id=1, source_target_pairs={{0,24},{1,25},{2,26},{3,27},{4,28},{5,29},{6,30},{7,31},{8,0},{9,1... | collective-permute-start | bytes 393224 | tf_op jit(solution)/shard_map/ppermute | solution.py:38
  24.1 0.7 %collective-permute-start.2 = (bf16[2,8,4096]{2,1,0:T(8,128)(2,1)S(1)}, bf16[2,8,4096]{2,1,0:T(8,128)(2,1)S(1)}, u32[]{:S(2)}, u32[]{:S(2)}) collective-permute-start(bf16[2,8,4096]{2,1,0:T(8,128)(2,1)S(1)} %pad_maximum_fusion.refs_0_), channel_id=1, source_target_pairs={{0,8},{1,9},{2,10},{3,11},{4,12},{5,13},{6,14},{7,15},{8,16},{9,17... | collective-permute-start | bytes 393224 | tf_op jit(solution)/shard_map/ppermute | solution.py:38
  25.4 4.4 %collective-permute-done.5.refs_5_ = s32[1,8]{1,0:T(1,128)S(1)} collective-permute-done((s32[1,8]{1,0:T(1,128)S(1)}, s32[1,8]{1,0:T(1,128)S(1)}, u32[]{:S(2)}, u32[]{:S(2)}) %collective-permute-start.5) | collective-permute-done | bytes 64 | tf_op jit(solution)/shard_map/ppermute | solution.py:38
  30.2 3.3 %collective-permute-done.2.refs_1_ = bf16[2,8,4096]{2,1,0:T(8,128)(2,1)S(1)} collective-permute-done((bf16[2,8,4096]{2,1,0:T(8,128)(2,1)S(1)}, bf16[2,8,4096]{2,1,0:T(8,128)(2,1)S(1)}, u32[]{:S(2)}, u32[]{:S(2)}) %collective-permute-start.2) | collective-permute-done | bytes 131104 | tf_op jit(solution)/shard_map/ppermute | solution.py:38
  33.5 0.7 %pick.1 = (bf16[2,8,8,512]{3,2,1,0:T(8,128)(2,1)S(1)}, bf16[2,8,8,512]{3,2,1,0:T(8,128)(2,1)S(1)}, bf16[2,8,8,512]{3,2,1,0:T(8,128)(2,1)S(1)}, bf16[2,8,8,512]{3,2,1,0:T(8,128)(2,1)S(1)}) custom-call(bf16[2,8,4096]{2,1,0:T(8,128)(2,1)S(1)} %pad_maximum_fusion.refs_0_, bf16[2,8,4096]{2,1,0:T(8,128)(2,1)S(1)} %collective-permute-done.2.refs_1_, ...), custom_call_target="tpu_custom_call" | custom-call | flops 21474836480 | bytes 1048576 | tf_op jit(solution)/shard_map/pick/pallas_call | solution.py:81
  34.2 0.8 %collective-permute-start.8 = (bf16[2,8,8,512]{3,2,1,0:T(8,128)(2,1)S(1)}, bf16[2,8,8,512]{3,2,1,0:T(8,128)(2,1)S(1)}, u32[]{:S(2)}, u32[]{:S(2)}) collective-permute-start(bf16[2,8,8,512]{3,2,1,0:T(8,128)(2,1)S(1)} %get-tuple-element.18), channel_id=1, source_target_pairs={{0,64},{1,193},{2,66},{3,195},{4,68},{5,197},{6,70},{7,199},{8,72}... | collective-permute-start | bytes 393224 | tf_op jit(solution)/shard_map/ppermute | solution.py:38
  35.0 2.7 %collective-permute-start.10 = (bf16[2,8,8,512]{3,2,1,0:T(8,128)(2,1)S(1)}, bf16[2,8,8,512]{3,2,1,0:T(8,128)(2,1)S(1)}, u32[]{:S(2)}, u32[]{:S(2)}) collective-permute-start(bf16[2,8,8,512]{3,2,1,0:T(8,128)(2,1)S(1)} %get-tuple-element.20), channel_id=1, source_target_pairs={{0,224},{1,225},{2,226},{3,227},{4,228},{5,229},{6,230},{7,231},{8... | collective-permute-start | bytes 393224 | tf_op jit(solution)/shard_map/ppermute | solution.py:38
  37.7 1.4 %near.1.refs_5_ = f32[64,4096]{1,0:T(8,128)S(1)} custom-call(bf16[2,8,512]{2,1,0:T(8,128)(2,1)S(1)} %maximum_bitcast_fusion.refs_0_, bf16[2,8,512]{2,1,0:T(8,128)(2,1)S(1)} %get-tuple-element.31.refs_1_, bf16[2,8,512]{2,1,0:T(8,128)(2,1)S(1)} %get-tuple-element.32.refs_2_, bf16[2,8,512]{2,1,0:T(8,128)(2,1)S(1)} %get-tuple-element.30.refs_3_, ...), custom_call_target="tpu_custom_call" | custom-call | flops 268435456 | bytes 5242880 | tf_op jit(solution)/shard_map/near/pallas_call | solution.py:131
  39.2 3.5 %collective-permute-done.9.refs_2_ = bf16[2,8,8,512]{3,2,1,0:T(8,128)(2,1)S(1)} collective-permute-done((bf16[2,8,8,512]{3,2,1,0:T(8,128)(2,1)S(1)}, bf16[2,8,8,512]{3,2,1,0:T(8,128)(2,1)S(1)}, u32[]{:S(2)}, u32[]{:S(2)}) %collective-permute-start.9) | collective-permute-done | bytes 131104 | tf_op jit(solution)/shard_map/ppermute | solution.py:38
  42.7 1.7 %product.1 = (f32[32,4096]{1,0:T(8,128)S(1)}, bf16[32,4096]{1,0:T(8,128)(2,1)S(1)}) custom-call(s32[8]{0:T(128)S(1)} %bitcast.20, bf16[2,8,8,512]{3,2,1,0:T(8,128)(2,1)S(1)} %get-tuple-element.17.refs_0_, bf16[2,8,8,512]{3,2,1,0:T(8,128)(2,1)S(1)} %collective-permute-done.8.refs_1_, bf16[2,8,8,512]{3,2,1,0:T(8,128)(2,1)S(1)} %collective-permute-done.9.refs_2_, ...), custom_call_target="tpu_custom_call" | custom-call | flops 536870912 | bytes 10485760 | tf_op jit(solution)/shard_map/product/pallas_call | solution.py:171
  44.4 1.2 %collective-permute-start.14 = (bf16[32,4096]{1,0:T(8,128)(2,1)S(1)}, bf16[32,4096]{1,0:T(8,128)(2,1)S(1)}, u32[]{:S(2)}, u32[]{:S(2)}) collective-permute-start(bf16[32,4096]{1,0:T(8,128)(2,1)S(1)} %get-tuple-element.24), channel_id=1, source_target_pairs={{0,1},{1,0},{2,3},{3,2},{4,5},{5,4},{6,7},{7,6},{8,9},{9,8},{10,11... | collective-permute-start | bytes 786440 | tf_op jit(solution)/shard_map/ppermute | solution.py:38
  45.6 1.2 %collective-permute-done.14 = bf16[32,4096]{1,0:T(8,128)(2,1)S(1)} collective-permute-done((bf16[32,4096]{1,0:T(8,128)(2,1)S(1)}, bf16[32,4096]{1,0:T(8,128)(2,1)S(1)}, u32[]{:S(2)}, u32[]{:S(2)}) %collective-permute-start.14) | collective-permute-done | bytes 262176 | tf_op jit(solution)/shard_map/ppermute | solution.py:38
  46.8 2.6 %collective-permute-start.15 = (bf16[8,4096]{1,0:T(8,128)(2,1)S(1)}, bf16[8,4096]{1,0:T(8,128)(2,1)S(1)}, u32[]{:S(2)}, u32[]{:S(2)}) collective-permute-start(bf16[8,4096]{1,0:T(8,128)(2,1)S(1)} %get-tuple-element.27), channel_id=1, source_target_pairs={{0,4},{1,5},{2,6},{3,7},{4,0},{5,1},{6,2},{7,3},{8,12},{9,13},{10,... | collective-permute-start | bytes 196616 | tf_op jit(solution)/shard_map/ppermute | solution.py:38
  49.5 0.9 %collective-permute-start.17 = (bf16[8,4096]{1,0:T(8,128)(2,1)S(1)}, bf16[8,4096]{1,0:T(8,128)(2,1)S(1)}, u32[]{:S(2)}, u32[]{:S(2)}) collective-permute-start(bf16[8,4096]{1,0:T(8,128)(2,1)S(1)} %get-tuple-element.28), channel_id=1, source_target_pairs={{0,6},{1,7},{2,4},{3,5},{4,2},{5,3},{6,0},{7,1},{8,14},{9,15},{10,... | collective-permute-start | bytes 196616 | tf_op jit(solution)/shard_map/ppermute | solution.py:38
  50.4 1.2 %collective-permute-done.15 = bf16[8,4096]{1,0:T(8,128)(2,1)S(1)} collective-permute-done((bf16[8,4096]{1,0:T(8,128)(2,1)S(1)}, bf16[8,4096]{1,0:T(8,128)(2,1)S(1)}, u32[]{:S(2)}, u32[]{:S(2)}) %collective-permute-start.15) | collective-permute-done | bytes 65568 | tf_op jit(solution)/shard_map/ppermute | solution.py:38
  51.6 2.2 %collective-permute-done.17 = bf16[8,4096]{1,0:T(8,128)(2,1)S(1)} collective-permute-done((bf16[8,4096]{1,0:T(8,128)(2,1)S(1)}, bf16[8,4096]{1,0:T(8,128)(2,1)S(1)}, u32[]{:S(2)}, u32[]{:S(2)}) %collective-permute-start.17) | collective-permute-done | bytes 65568 | tf_op jit(solution)/shard_map/ppermute | solution.py:38
  53.8 0.7 %fusion.2 = bf16[8,4096]{1,0:T(8,128)(2,1)} fusion(f32[32,4096]{1,0:T(8,128)S(1)} %get-tuple-element.26, bf16[8,4096]{1,0:T(8,128)(2,1)S(1)} %collective-permute-done.17, bf16[8,4096]{1,0:T(8,128)(2,1)S(1)} %collective-permute-done.16, bf16[8,4096]{1,0:T(8,128)(2,1)S(1)} %collective-permute-done.15), kind=kLoop, calls=%fused_computation.4 | loop fusion | flops 229376 | bytes 393216 | tf_op jit(solution)/shard_map/convert_element_type | solution.py:201
  (35 shorter events, 1.6 us)
Async XLA Ops:
  0.0 18.3 %copy-start.4 = (s32[1,8]{1,0:T(1,128)S(1)}, s32[1,8]{1,0:T(1,128)}, u32[]{:S(2)}) copy-start(s32[1,8]{1,0:T(1,128)} %refs_4_.1) | copy-start | bytes 100
  0.9 10.7 %collective-permute-start.11 = (bf16[4,8,512]{2,1,0:T(8,128)(2,1)S(1)}, bf16[4,8,512]{2,1,0:T(8,128)(2,1)S(1)}, u32[]{:S(2)}, u32[]{:S(2)}) collective-permute-start(bf16[4,8,512]{2,1,0:T(8,128)(2,1)S(1)} %get-tuple-element.22), channel_id=1, source_target_pairs={{0,1},{1,0},{2,3},{3,2},{4,5},{5,4},{6,7},{7,6},{8,9},{9,8},{10,11... | collective-permute-start | bytes 98312 | tf_op jit(solution)/shard_map/ppermute | solution.py:38
  4.1 9.4 %collective-permute-start = (bf16[8,4096]{1,0:T(8,128)(2,1)}, bf16[8,4096]{1,0:T(8,128)(2,1)S(1)}, u32[]{:S(2)}, u32[]{:S(2)}) collective-permute-start(bf16[8,4096]{1,0:T(8,128)(2,1)} %x_ref.1), channel_id=1, source_target_pairs={{0,0},{1,32},{2,64},{3,96},{4,128},{5,160},{6,192},{7,224},{8,8},{... | collective-permute-start | bytes 196616 | tf_op jit(solution)/shard_map/ppermute | solution.py:38
  6.0 12.2 %collective-permute-start.1 = (bf16[8,4096]{1,0:T(8,128)(2,1)}, bf16[8,4096]{1,0:T(8,128)(2,1)S(1)}, u32[]{:S(2)}, u32[]{:S(2)}) collective-permute-start(bf16[8,4096]{1,0:T(8,128)(2,1)} %x_ref.1), channel_id=1, source_target_pairs={{0,128},{1,160},{2,192},{3,224},{4,0},{5,32},{6,64},{7,96},{8,136}... | collective-permute-start | bytes 196616 | tf_op jit(solution)/shard_map/ppermute | solution.py:38
  11.6 12.6 %collective-permute-start.12 = (bf16[2,2,8,512]{3,2,1,0:T(8,128)(2,1)S(1)}, bf16[2,2,8,512]{3,2,1,0:T(8,128)(2,1)S(1)}, u32[]{:S(2)}, u32[]{:S(2)}) collective-permute-start(bf16[2,2,8,512]{3,2,1,0:T(8,128)(2,1)S(1)} %pad_maximum_fusion.1), channel_id=1, source_target_pairs={{0,4},{1,5},{2,6},{3,7},{4,0},{5,1},{6,2},{7,3},{8,12},{9,13},{10,... | collective-permute-start | bytes 98312 | tf_op jit(solution)/shard_map/ppermute | solution.py:38
  18.3 6.6 %collective-permute-start.7 = (s32[1,8]{1,0:T(1,128)S(1)}, s32[1,8]{1,0:T(1,128)S(1)}, u32[]{:S(2)}, u32[]{:S(2)}) collective-permute-start(s32[1,8]{1,0:T(1,128)S(1)} %copy-done.4), channel_id=1, source_target_pairs={{0,32},{1,33},{2,34},{3,35},{4,36},{5,37},{6,38},{7,39},{8,40},{9,... | collective-permute-start | bytes 104 | tf_op jit(solution)/shard_map/ppermute | solution.py:38
  18.4 6.6 %collective-permute-start.6 = (s32[1,8]{1,0:T(1,128)S(1)}, s32[1,8]{1,0:T(1,128)S(1)}, u32[]{:S(2)}, u32[]{:S(2)}) collective-permute-start(s32[1,8]{1,0:T(1,128)S(1)} %copy-done.4), channel_id=1, source_target_pairs={{0,224},{1,225},{2,226},{3,227},{4,228},{5,229},{6,230},{7,231},{8... | collective-permute-start | bytes 104 | tf_op jit(solution)/shard_map/ppermute | solution.py:38
  21.0 8.7 %collective-permute-start.4 = (bf16[2,8,4096]{2,1,0:T(8,128)(2,1)S(1)}, bf16[2,8,4096]{2,1,0:T(8,128)(2,1)S(1)}, u32[]{:S(2)}, u32[]{:S(2)}) collective-permute-start(bf16[2,8,4096]{2,1,0:T(8,128)(2,1)S(1)} %pad_maximum_fusion.refs_0_), channel_id=1, source_target_pairs={{0,24},{1,25},{2,26},{3,27},{4,28},{5,29},{6,30},{7,31},{8,0},{9,1... | collective-permute-start | bytes 393224 | tf_op jit(solution)/shard_map/ppermute | solution.py:38
  23.8 6.4 %collective-permute-start.3 = (bf16[2,8,4096]{2,1,0:T(8,128)(2,1)S(1)}, bf16[2,8,4096]{2,1,0:T(8,128)(2,1)S(1)}, u32[]{:S(2)}, u32[]{:S(2)}) collective-permute-start(bf16[2,8,4096]{2,1,0:T(8,128)(2,1)S(1)} %pad_maximum_fusion.refs_0_), channel_id=1, source_target_pairs={{0,16},{1,17},{2,18},{3,19},{4,20},{5,21},{6,22},{7,23},{8,24},{9,... | collective-permute-start | bytes 393224 | tf_op jit(solution)/shard_map/ppermute | solution.py:38
  24.1 9.4 %collective-permute-start.2 = (bf16[2,8,4096]{2,1,0:T(8,128)(2,1)S(1)}, bf16[2,8,4096]{2,1,0:T(8,128)(2,1)S(1)}, u32[]{:S(2)}, u32[]{:S(2)}) collective-permute-start(bf16[2,8,4096]{2,1,0:T(8,128)(2,1)S(1)} %pad_maximum_fusion.refs_0_), channel_id=1, source_target_pairs={{0,8},{1,9},{2,10},{3,11},{4,12},{5,13},{6,14},{7,15},{8,16},{9,17... | collective-permute-start | bytes 393224 | tf_op jit(solution)/shard_map/ppermute | solution.py:38
  24.8 12.8 %copy-start.1 = (bf16[4096,512]{1,0:T(8,128)(2,1)S(1)}, bf16[4096,512]{1,0:T(8,128)(2,1)}, u32[]{:S(2)}) copy-start(bf16[4096,512]{1,0:T(8,128)(2,1)} %refs_4_.2) | copy-start | bytes 12582916
  24.9 4.9 %collective-permute-start.5 = (s32[1,8]{1,0:T(1,128)S(1)}, s32[1,8]{1,0:T(1,128)S(1)}, u32[]{:S(2)}, u32[]{:S(2)}) collective-permute-start(s32[1,8]{1,0:T(1,128)S(1)} %copy-done.4), channel_id=1, source_target_pairs={{0,192},{1,65},{2,194},{3,67},{4,196},{5,69},{6,198},{7,71},{8,200... | collective-permute-start | bytes 104 | tf_op jit(solution)/shard_map/ppermute | solution.py:38
  25.0 12.7 %collective-permute-start.13 = (bf16[2,2,8,512]{3,2,1,0:T(8,128)(2,1)S(1)}, bf16[2,2,8,512]{3,2,1,0:T(8,128)(2,1)S(1)}, u32[]{:S(2)}, u32[]{:S(2)}) collective-permute-start(bf16[2,2,8,512]{3,2,1,0:T(8,128)(2,1)S(1)} %fusion.6), channel_id=1, source_target_pairs={{0,2},{1,3},{2,0},{3,1},{4,6},{5,7},{6,4},{7,5},{8,10},{9,11},{10,... | collective-permute-start | bytes 98312 | tf_op jit(solution)/shard_map/ppermute | solution.py:38
  34.2 8.5 %copy-start = (bf16[1,8,64,4096]{3,2,1,0:T(8,128)(2,1)S(1)}, bf16[1,8,64,4096]{3,2,1,0:T(8,128)(2,1)}, u32[]{:S(2)}) copy-start(bf16[1,8,64,4096]{3,2,1,0:T(8,128)(2,1)} %param.8) | copy-start | bytes 12582916
  34.2 8.5 %copy-start.2 = (bf16[1,8,64,512]{3,2,1,0:T(8,128)(2,1)S(1)}, bf16[1,8,64,512]{3,2,1,0:T(8,128)(2,1)}, u32[]{:S(2)}) copy-start(bf16[1,8,64,512]{3,2,1,0:T(8,128)(2,1)} %param.7) | copy-start | bytes 1572868
  34.2 8.5 %copy-start.3 = (s32[1,8]{1,0:T(1,128)S(1)}, s32[1,8]{1,0:T(1,128)}, u32[]{:S(2)}) copy-start(s32[1,8]{1,0:T(1,128)} %param.10) | copy-start | bytes 100
  34.2 4.9 %collective-permute-start.8 = (bf16[2,8,8,512]{3,2,1,0:T(8,128)(2,1)S(1)}, bf16[2,8,8,512]{3,2,1,0:T(8,128)(2,1)S(1)}, u32[]{:S(2)}, u32[]{:S(2)}) collective-permute-start(bf16[2,8,8,512]{3,2,1,0:T(8,128)(2,1)S(1)} %get-tuple-element.18), channel_id=1, source_target_pairs={{0,64},{1,193},{2,66},{3,195},{4,68},{5,197},{6,70},{7,199},{8,72}... | collective-permute-start | bytes 393224 | tf_op jit(solution)/shard_map/ppermute | solution.py:38
  35.0 7.7 %collective-permute-start.9 = (bf16[2,8,8,512]{3,2,1,0:T(8,128)(2,1)S(1)}, bf16[2,8,8,512]{3,2,1,0:T(8,128)(2,1)S(1)}, u32[]{:S(2)}, u32[]{:S(2)}) collective-permute-start(bf16[2,8,8,512]{3,2,1,0:T(8,128)(2,1)S(1)} %get-tuple-element.19), channel_id=1, source_target_pairs={{0,32},{1,33},{2,34},{3,35},{4,36},{5,37},{6,38},{7,39},{8,40},{9,... | collective-permute-start | bytes 393224 | tf_op jit(solution)/shard_map/ppermute | solution.py:38
  35.0 7.7 %collective-permute-start.10 = (bf16[2,8,8,512]{3,2,1,0:T(8,128)(2,1)S(1)}, bf16[2,8,8,512]{3,2,1,0:T(8,128)(2,1)S(1)}, u32[]{:S(2)}, u32[]{:S(2)}) collective-permute-start(bf16[2,8,8,512]{3,2,1,0:T(8,128)(2,1)S(1)} %get-tuple-element.20), channel_id=1, source_target_pairs={{0,224},{1,225},{2,226},{3,227},{4,228},{5,229},{6,230},{7,231},{8... | collective-permute-start | bytes 393224 | tf_op jit(solution)/shard_map/ppermute | solution.py:38
  44.4 2.4 %collective-permute-start.14 = (bf16[32,4096]{1,0:T(8,128)(2,1)S(1)}, bf16[32,4096]{1,0:T(8,128)(2,1)S(1)}, u32[]{:S(2)}, u32[]{:S(2)}) collective-permute-start(bf16[32,4096]{1,0:T(8,128)(2,1)S(1)} %get-tuple-element.24), channel_id=1, source_target_pairs={{0,1},{1,0},{2,3},{3,2},{4,5},{5,4},{6,7},{7,6},{8,9},{9,8},{10,11... | collective-permute-start | bytes 786440 | tf_op jit(solution)/shard_map/ppermute | solution.py:38
  46.8 4.7 %collective-permute-start.15 = (bf16[8,4096]{1,0:T(8,128)(2,1)S(1)}, bf16[8,4096]{1,0:T(8,128)(2,1)S(1)}, u32[]{:S(2)}, u32[]{:S(2)}) collective-permute-start(bf16[8,4096]{1,0:T(8,128)(2,1)S(1)} %get-tuple-element.27), channel_id=1, source_target_pairs={{0,4},{1,5},{2,6},{3,7},{4,0},{5,1},{6,2},{7,3},{8,12},{9,13},{10,... | collective-permute-start | bytes 196616 | tf_op jit(solution)/shard_map/ppermute | solution.py:38
  49.5 4.3 %collective-permute-start.17 = (bf16[8,4096]{1,0:T(8,128)(2,1)S(1)}, bf16[8,4096]{1,0:T(8,128)(2,1)S(1)}, u32[]{:S(2)}, u32[]{:S(2)}) collective-permute-start(bf16[8,4096]{1,0:T(8,128)(2,1)S(1)} %get-tuple-element.28), channel_id=1, source_target_pairs={{0,6},{1,7},{2,4},{3,5},{4,2},{5,3},{6,0},{7,1},{8,14},{9,15},{10,... | collective-permute-start | bytes 196616 | tf_op jit(solution)/shard_map/ppermute | solution.py:38
  50.4 3.4 %collective-permute-start.16 = (bf16[8,4096]{1,0:T(8,128)(2,1)S(1)}, bf16[8,4096]{1,0:T(8,128)(2,1)S(1)}, u32[]{:S(2)}, u32[]{:S(2)}) collective-permute-start(bf16[8,4096]{1,0:T(8,128)(2,1)S(1)} %get-tuple-element.29), channel_id=1, source_target_pairs={{0,2},{1,3},{2,0},{3,1},{4,6},{5,7},{6,4},{7,5},{8,10},{9,11},{10,... | collective-permute-start | bytes 196616 | tf_op jit(solution)/shard_map/ppermute | solution.py:38

commit v4 on v3

--- a/solution.py
+++ b/solution.py
@@ -14,6 +14,7 @@
 VMEM, SMEM = pl.BlockSpec(memory_space=pltpu.VMEM), pl.BlockSpec(memory_space=pltpu.SMEM)
 TURNS = (0, 4)
 SENDS = ((0, (0, 1)), (2, (0, 1)), (1, (0, 1)), (-1, (0, 1)))
+UPS = (0, 1, 3, 2)
 LONG = pl.CostEstimate(flops=20 << 30, bytes_accessed=1 << 20, transcendentals=0)
 LIMIT = pltpu.CompilerParams(vmem_limit_bytes=8 << 20)
 
@@ -66,8 +67,8 @@
     n = len(SENDS)
     held_refs, asked_refs, out_refs, held_ref = refs[:Y], refs[Y:Y + n], refs[Y + n:-1], refs[-1]
     y, core = lax.axis_index("rows") & 3, lax.axis_index("rhs") & 1
-    for m in range(Y):
-        held_ref[m] = held_refs[m][...]
+    for m, ref in zip(UPS, held_refs):
+        held_ref[m] = ref[...]
     for (way, parts), asked_ref, out_ref in zip(SENDS, asked_refs, out_refs):
         for b in range(BLK):
             piece = asked_ref[0, b]
@@ -187,7 +188,7 @@
     own = own_piece(*halves(x_t))
     both, asked = lax.optimization_barrier((both, far_cols))
     asked = [asked if way == 0 else ask_z(asked, way) for way, _ in SENDS]
-    sent = pick([along_y(both, m) for m in range(Y)], asked)
+    sent = pick([along_y(both, m) for m in UPS], asked)
     got = [part if way == 0 else send_z(part, way) for part, (way, _) in zip(sent, SENDS)]
     near = near_product(own, near_block)
     keep, send = product(

time: 54.6 us -> 53.7 us (0.984)
  waiting for transfers between devices: 21.1 us -> 17 us
  starting transfers between devices: 27.8 us -> 30.9 us
    ppermute x18, waiting for transfers between devices: 21.1 us -> 17 us  [move(): return lax.ppermute(part, AXES, pairs(target))]
    ppermute x18, starting transfers between devices: 27.8 us -> 30.9 us  [move(): return lax.ppermute(part, AXES, pairs(target))]
  transfers between devices with their start and end apart: 18 -> 18, of which waited for: 9 -> 8; matrix products, arithmetic and copies ran while one was open for 0% -> 0% of each run, Pallas kernels for 4% -> 4%
where the time goes in v4:
time: 53.7 us; the launch traced here: 53.5 us
  starting transfers between devices  30.9 us (58%)
  waiting for transfers between devices  17 us (32%)
  Pallas kernels  4.6 us (9%)
  other arithmetic  0.75 us (1%)
    ppermute x18, starting transfers between devices, move(): return lax.ppermute(part, AXES, pairs(target))  30.9 us
    ppermute x18, waiting for transfers between devices, move(): return lax.ppermute(part, AXES, pairs(target))  17 us
    pallas_call x1, Pallas kernels, product(): pl.pallas_call(product_kernel, out_shape=(f32(32, S), bf16(32, S)), in_sp...  1.69 us
    pallas_call x1, Pallas kernels, near_product(): pl.pallas_call(near_kernel, out_shape=f32(64, S), in_specs=[VMEM] * (X +...  1.37 us
  transfers between devices with their start and end apart: 18, of which 8 were waited for; matrix products, arithmetic and copies ran while one was open for 0% of the time, Pallas kernels for 4%

profile of v4, /device:TPU:1, one launch (start us, length us, event | category | flops | bytes accessed | tf_op | source)
XLA Modules:
  0.0 53.5 jit_solution(9935688663334524487)
XLA Ops:
  0.0 0.9 %halves.1 = (bf16[4,8,512]{2,1,0:T(8,128)(2,1)S(1)}, bf16[4,8,512]{2,1,0:T(8,128)(2,1)S(1)}) custom-call(bf16[8,4096]{1,0:T(8,128)(2,1)} %x_ref.1), custom_call_target="tpu_custom_call" | custom-call | flops 21474836480 | bytes 1048576 | tf_op jit(solution)/shard_map/halves/pallas_call | solution.py:104
  0.9 3.2 %collective-permute-start.11 = (bf16[4,8,512]{2,1,0:T(8,128)(2,1)S(1)}, bf16[4,8,512]{2,1,0:T(8,128)(2,1)S(1)}, u32[]{:S(2)}, u32[]{:S(2)}) collective-permute-start(bf16[4,8,512]{2,1,0:T(8,128)(2,1)S(1)} %get-tuple-element.22), channel_id=1, source_target_pairs={{0,1},{1,0},{2,3},{3,2},{4,5},{5,4},{6,7},{7,6},{8,9},{9,8},{10,11... | collective-permute-start | bytes 98312 | tf_op jit(solution)/shard_map/ppermute | solution.py:39
  4.1 1.9 %collective-permute-start = (bf16[8,4096]{1,0:T(8,128)(2,1)}, bf16[8,4096]{1,0:T(8,128)(2,1)S(1)}, u32[]{:S(2)}, u32[]{:S(2)}) collective-permute-start(bf16[8,4096]{1,0:T(8,128)(2,1)} %x_ref.1), channel_id=1, source_target_pairs={{0,0},{1,32},{2,64},{3,96},{4,128},{5,160},{6,192},{7,224},{8,8},{... | collective-permute-start | bytes 196616 | tf_op jit(solution)/shard_map/ppermute | solution.py:39
  6.0 5.5 %collective-permute-start.1 = (bf16[8,4096]{1,0:T(8,128)(2,1)}, bf16[8,4096]{1,0:T(8,128)(2,1)S(1)}, u32[]{:S(2)}, u32[]{:S(2)}) collective-permute-start(bf16[8,4096]{1,0:T(8,128)(2,1)} %x_ref.1), channel_id=1, source_target_pairs={{0,128},{1,160},{2,192},{3,224},{4,0},{5,32},{6,64},{7,96},{8,136}... | collective-permute-start | bytes 196616 | tf_op jit(solution)/shard_map/ppermute | solution.py:39
  11.6 2.0 %collective-permute-start.12 = (bf16[2,2,8,512]{3,2,1,0:T(8,128)(2,1)S(1)}, bf16[2,2,8,512]{3,2,1,0:T(8,128)(2,1)S(1)}, u32[]{:S(2)}, u32[]{:S(2)}) collective-permute-start(bf16[2,2,8,512]{3,2,1,0:T(8,128)(2,1)S(1)} %pad_maximum_fusion.1), channel_id=1, source_target_pairs={{0,4},{1,5},{2,6},{3,7},{4,0},{5,1},{6,2},{7,3},{8,12},{9,13},{10,... | collective-permute-start | bytes 98312 | tf_op jit(solution)/shard_map/ppermute | solution.py:39
  13.5 4.7 %collective-permute-done.1 = bf16[8,4096]{1,0:T(8,128)(2,1)S(1)} collective-permute-done((bf16[8,4096]{1,0:T(8,128)(2,1)}, bf16[8,4096]{1,0:T(8,128)(2,1)S(1)}, u32[]{:S(2)}, u32[]{:S(2)}) %collective-permute-start.1) | collective-permute-done | bytes 65568 | tf_op jit(solution)/shard_map/ppermute | solution.py:39
  18.4 2.7 %collective-permute-start.6 = (s32[1,8]{1,0:T(1,128)S(1)}, s32[1,8]{1,0:T(1,128)S(1)}, u32[]{:S(2)}, u32[]{:S(2)}) collective-permute-start(s32[1,8]{1,0:T(1,128)S(1)} %copy-done.4), channel_id=1, source_target_pairs={{0,224},{1,225},{2,226},{3,227},{4,228},{5,229},{6,230},{7,231},{8... | collective-permute-start | bytes 104 | tf_op jit(solution)/shard_map/ppermute | solution.py:39
  21.0 2.9 %collective-permute-start.4 = (bf16[2,8,4096]{2,1,0:T(8,128)(2,1)S(1)}, bf16[2,8,4096]{2,1,0:T(8,128)(2,1)S(1)}, u32[]{:S(2)}, u32[]{:S(2)}) collective-permute-start(bf16[2,8,4096]{2,1,0:T(8,128)(2,1)S(1)} %pad_maximum_fusion.refs_0_), channel_id=1, source_target_pairs={{0,16},{1,17},{2,18},{3,19},{4,20},{5,21},{6,22},{7,23},{8,24},{9,... | collective-permute-start | bytes 393224 | tf_op jit(solution)/shard_map/ppermute | solution.py:39
  24.0 0.8 %collective-permute-start.3 = (bf16[2,8,4096]{2,1,0:T(8,128)(2,1)S(1)}, bf16[2,8,4096]{2,1,0:T(8,128)(2,1)S(1)}, u32[]{:S(2)}, u32[]{:S(2)}) collective-permute-start(bf16[2,8,4096]{2,1,0:T(8,128)(2,1)S(1)} %pad_maximum_fusion.refs_0_), channel_id=1, source_target_pairs={{0,24},{1,25},{2,26},{3,27},{4,28},{5,29},{6,30},{7,31},{8,0},{9,1... | collective-permute-start | bytes 393224 | tf_op jit(solution)/shard_map/ppermute | solution.py:39
  24.7 0.7 %collective-permute-start.2 = (bf16[2,8,4096]{2,1,0:T(8,128)(2,1)S(1)}, bf16[2,8,4096]{2,1,0:T(8,128)(2,1)S(1)}, u32[]{:S(2)}, u32[]{:S(2)}) collective-permute-start(bf16[2,8,4096]{2,1,0:T(8,128)(2,1)S(1)} %pad_maximum_fusion.refs_0_), channel_id=1, source_target_pairs={{0,8},{1,9},{2,10},{3,11},{4,12},{5,13},{6,14},{7,15},{8,16},{9,17... | collective-permute-start | bytes 393224 | tf_op jit(solution)/shard_map/ppermute | solution.py:39
  26.0 4.1 %collective-permute-done.5.refs_5_ = s32[1,8]{1,0:T(1,128)S(1)} collective-permute-done((s32[1,8]{1,0:T(1,128)S(1)}, s32[1,8]{1,0:T(1,128)S(1)}, u32[]{:S(2)}, u32[]{:S(2)}) %collective-permute-start.5) | collective-permute-done | bytes 64 | tf_op jit(solution)/shard_map/ppermute | solution.py:39
  30.0 0.9 %collective-permute-done.3.refs_2_ = bf16[2,8,4096]{2,1,0:T(8,128)(2,1)S(1)} collective-permute-done((bf16[2,8,4096]{2,1,0:T(8,128)(2,1)S(1)}, bf16[2,8,4096]{2,1,0:T(8,128)(2,1)S(1)}, u32[]{:S(2)}, u32[]{:S(2)}) %collective-permute-start.3) | collective-permute-done | bytes 131104 | tf_op jit(solution)/shard_map/ppermute | solution.py:39
  30.9 0.7 %pick.1 = (bf16[2,8,8,512]{3,2,1,0:T(8,128)(2,1)S(1)}, bf16[2,8,8,512]{3,2,1,0:T(8,128)(2,1)S(1)}, bf16[2,8,8,512]{3,2,1,0:T(8,128)(2,1)S(1)}, bf16[2,8,8,512]{3,2,1,0:T(8,128)(2,1)S(1)}) custom-call(bf16[2,8,4096]{2,1,0:T(8,128)(2,1)S(1)} %pad_maximum_fusion.refs_0_, bf16[2,8,4096]{2,1,0:T(8,128)(2,1)S(1)} %collective-permute-done.2.refs_1_, ...), custom_call_target="tpu_custom_call" | custom-call | flops 21474836480 | bytes 1048576 | tf_op jit(solution)/shard_map/pick/pallas_call | solution.py:82
  31.6 0.6 %collective-permute-start.8 = (bf16[2,8,8,512]{3,2,1,0:T(8,128)(2,1)S(1)}, bf16[2,8,8,512]{3,2,1,0:T(8,128)(2,1)S(1)}, u32[]{:S(2)}, u32[]{:S(2)}) collective-permute-start(bf16[2,8,8,512]{3,2,1,0:T(8,128)(2,1)S(1)} %get-tuple-element.18), channel_id=1, source_target_pairs={{0,64},{1,193},{2,66},{3,195},{4,68},{5,197},{6,70},{7,199},{8,72}... | collective-permute-start | bytes 393224 | tf_op jit(solution)/shard_map/ppermute | solution.py:39
  32.2 2.7 %collective-permute-start.10 = (bf16[2,8,8,512]{3,2,1,0:T(8,128)(2,1)S(1)}, bf16[2,8,8,512]{3,2,1,0:T(8,128)(2,1)S(1)}, u32[]{:S(2)}, u32[]{:S(2)}) collective-permute-start(bf16[2,8,8,512]{3,2,1,0:T(8,128)(2,1)S(1)} %get-tuple-element.20), channel_id=1, source_target_pairs={{0,224},{1,225},{2,226},{3,227},{4,228},{5,229},{6,230},{7,231},{8... | collective-permute-start | bytes 393224 | tf_op jit(solution)/shard_map/ppermute | solution.py:39
  34.9 1.4 %near.1.refs_5_ = f32[64,4096]{1,0:T(8,128)S(1)} custom-call(bf16[2,8,512]{2,1,0:T(8,128)(2,1)S(1)} %maximum_bitcast_fusion.refs_0_, bf16[2,8,512]{2,1,0:T(8,128)(2,1)S(1)} %get-tuple-element.31.refs_1_, bf16[2,8,512]{2,1,0:T(8,128)(2,1)S(1)} %get-tuple-element.32.refs_2_, bf16[2,8,512]{2,1,0:T(8,128)(2,1)S(1)} %get-tuple-element.30.refs_3_, ...), custom_call_target="tpu_custom_call" | custom-call | flops 268435456 | bytes 5242880 | tf_op jit(solution)/shard_map/near/pallas_call | solution.py:132
  36.7 1.9 %collective-permute-done.9.refs_2_ = bf16[2,8,8,512]{3,2,1,0:T(8,128)(2,1)S(1)} collective-permute-done((bf16[2,8,8,512]{3,2,1,0:T(8,128)(2,1)S(1)}, bf16[2,8,8,512]{3,2,1,0:T(8,128)(2,1)S(1)}, u32[]{:S(2)}, u32[]{:S(2)}) %collective-permute-start.9) | collective-permute-done | bytes 131104 | tf_op jit(solution)/shard_map/ppermute | solution.py:39
  38.6 1.7 %product.1 = (f32[32,4096]{1,0:T(8,128)S(1)}, bf16[32,4096]{1,0:T(8,128)(2,1)S(1)}) custom-call(s32[8]{0:T(128)S(1)} %bitcast.20, bf16[2,8,8,512]{3,2,1,0:T(8,128)(2,1)S(1)} %get-tuple-element.17.refs_0_, bf16[2,8,8,512]{3,2,1,0:T(8,128)(2,1)S(1)} %collective-permute-done.8.refs_1_, bf16[2,8,8,512]{3,2,1,0:T(8,128)(2,1)S(1)} %collective-permute-done.9.refs_2_, ...), custom_call_target="tpu_custom_call" | custom-call | flops 536870912 | bytes 10485760 | tf_op jit(solution)/shard_map/product/pallas_call | solution.py:172
  40.3 3.2 %collective-permute-start.14 = (bf16[32,4096]{1,0:T(8,128)(2,1)S(1)}, bf16[32,4096]{1,0:T(8,128)(2,1)S(1)}, u32[]{:S(2)}, u32[]{:S(2)}) collective-permute-start(bf16[32,4096]{1,0:T(8,128)(2,1)S(1)} %get-tuple-element.24), channel_id=1, source_target_pairs={{0,1},{1,0},{2,3},{3,2},{4,5},{5,4},{6,7},{7,6},{8,9},{9,8},{10,11... | collective-permute-start | bytes 786440 | tf_op jit(solution)/shard_map/ppermute | solution.py:39
  43.6 1.2 %collective-permute-done.14 = bf16[32,4096]{1,0:T(8,128)(2,1)S(1)} collective-permute-done((bf16[32,4096]{1,0:T(8,128)(2,1)S(1)}, bf16[32,4096]{1,0:T(8,128)(2,1)S(1)}, u32[]{:S(2)}, u32[]{:S(2)}) %collective-permute-start.14) | collective-permute-done | bytes 262176 | tf_op jit(solution)/shard_map/ppermute | solution.py:39
  44.8 3.7 %collective-permute-start.15 = (bf16[8,4096]{1,0:T(8,128)(2,1)S(1)}, bf16[8,4096]{1,0:T(8,128)(2,1)S(1)}, u32[]{:S(2)}, u32[]{:S(2)}) collective-permute-start(bf16[8,4096]{1,0:T(8,128)(2,1)S(1)} %get-tuple-element.27), channel_id=1, source_target_pairs={{0,4},{1,5},{2,6},{3,7},{4,0},{5,1},{6,2},{7,3},{8,12},{9,13},{10,... | collective-permute-start | bytes 196616 | tf_op jit(solution)/shard_map/ppermute | solution.py:39
  48.9 1.7 %collective-permute-done.15 = bf16[8,4096]{1,0:T(8,128)(2,1)S(1)} collective-permute-done((bf16[8,4096]{1,0:T(8,128)(2,1)S(1)}, bf16[8,4096]{1,0:T(8,128)(2,1)S(1)}, u32[]{:S(2)}, u32[]{:S(2)}) %collective-permute-start.15) | collective-permute-done | bytes 65568 | tf_op jit(solution)/shard_map/ppermute | solution.py:39
  50.7 2.2 %collective-permute-done.17 = bf16[8,4096]{1,0:T(8,128)(2,1)S(1)} collective-permute-done((bf16[8,4096]{1,0:T(8,128)(2,1)S(1)}, bf16[8,4096]{1,0:T(8,128)(2,1)S(1)}, u32[]{:S(2)}, u32[]{:S(2)}) %collective-permute-start.17) | collective-permute-done | bytes 65568 | tf_op jit(solution)/shard_map/ppermute | solution.py:39
  52.8 0.7 %fusion.2 = bf16[8,4096]{1,0:T(8,128)(2,1)} fusion(f32[32,4096]{1,0:T(8,128)S(1)} %get-tuple-element.26, bf16[8,4096]{1,0:T(8,128)(2,1)S(1)} %collective-permute-done.17, bf16[8,4096]{1,0:T(8,128)(2,1)S(1)} %collective-permute-done.16, bf16[8,4096]{1,0:T(8,128)(2,1)S(1)} %collective-permute-done.15), kind=kLoop, calls=%fused_computation.4 | loop fusion | flops 229376 | bytes 393216 | tf_op jit(solution)/shard_map/convert_element_type | solution.py:202
  (35 shorter events, 1.6 us)
Async XLA Ops:
  0.0 18.3 %copy-start.4 = (s32[1,8]{1,0:T(1,128)S(1)}, s32[1,8]{1,0:T(1,128)}, u32[]{:S(2)}) copy-start(s32[1,8]{1,0:T(1,128)} %refs_4_.1) | copy-start | bytes 100
  0.9 10.7 %collective-permute-start.11 = (bf16[4,8,512]{2,1,0:T(8,128)(2,1)S(1)}, bf16[4,8,512]{2,1,0:T(8,128)(2,1)S(1)}, u32[]{:S(2)}, u32[]{:S(2)}) collective-permute-start(bf16[4,8,512]{2,1,0:T(8,128)(2,1)S(1)} %get-tuple-element.22), channel_id=1, source_target_pairs={{0,1},{1,0},{2,3},{3,2},{4,5},{5,4},{6,7},{7,6},{8,9},{9,8},{10,11... | collective-permute-start | bytes 98312 | tf_op jit(solution)/shard_map/ppermute | solution.py:39
  4.1 9.4 %collective-permute-start = (bf16[8,4096]{1,0:T(8,128)(2,1)}, bf16[8,4096]{1,0:T(8,128)(2,1)S(1)}, u32[]{:S(2)}, u32[]{:S(2)}) collective-permute-start(bf16[8,4096]{1,0:T(8,128)(2,1)} %x_ref.1), channel_id=1, source_target_pairs={{0,0},{1,32},{2,64},{3,96},{4,128},{5,160},{6,192},{7,224},{8,8},{... | collective-permute-start | bytes 196616 | tf_op jit(solution)/shard_map/ppermute | solution.py:39
  6.0 12.2 %collective-permute-start.1 = (bf16[8,4096]{1,0:T(8,128)(2,1)}, bf16[8,4096]{1,0:T(8,128)(2,1)S(1)}, u32[]{:S(2)}, u32[]{:S(2)}) collective-permute-start(bf16[8,4096]{1,0:T(8,128)(2,1)} %x_ref.1), channel_id=1, source_target_pairs={{0,128},{1,160},{2,192},{3,224},{4,0},{5,32},{6,64},{7,96},{8,136}... | collective-permute-start | bytes 196616 | tf_op jit(solution)/shard_map/ppermute | solution.py:39
  11.6 13.2 %collective-permute-start.12 = (bf16[2,2,8,512]{3,2,1,0:T(8,128)(2,1)S(1)}, bf16[2,2,8,512]{3,2,1,0:T(8,128)(2,1)S(1)}, u32[]{:S(2)}, u32[]{:S(2)}) collective-permute-start(bf16[2,2,8,512]{3,2,1,0:T(8,128)(2,1)S(1)} %pad_maximum_fusion.1), channel_id=1, source_target_pairs={{0,4},{1,5},{2,6},{3,7},{4,0},{5,1},{6,2},{7,3},{8,12},{9,13},{10,... | collective-permute-start | bytes 98312 | tf_op jit(solution)/shard_map/ppermute | solution.py:39
  18.3 7.2 %collective-permute-start.7 = (s32[1,8]{1,0:T(1,128)S(1)}, s32[1,8]{1,0:T(1,128)S(1)}, u32[]{:S(2)}, u32[]{:S(2)}) collective-permute-start(s32[1,8]{1,0:T(1,128)S(1)} %copy-done.4), channel_id=1, source_target_pairs={{0,32},{1,33},{2,34},{3,35},{4,36},{5,37},{6,38},{7,39},{8,40},{9,... | collective-permute-start | bytes 104 | tf_op jit(solution)/shard_map/ppermute | solution.py:39
  18.4 7.2 %collective-permute-start.6 = (s32[1,8]{1,0:T(1,128)S(1)}, s32[1,8]{1,0:T(1,128)S(1)}, u32[]{:S(2)}, u32[]{:S(2)}) collective-permute-start(s32[1,8]{1,0:T(1,128)S(1)} %copy-done.4), channel_id=1, source_target_pairs={{0,224},{1,225},{2,226},{3,227},{4,228},{5,229},{6,230},{7,231},{8... | collective-permute-start | bytes 104 | tf_op jit(solution)/shard_map/ppermute | solution.py:39
  21.0 9.0 %collective-permute-start.4 = (bf16[2,8,4096]{2,1,0:T(8,128)(2,1)S(1)}, bf16[2,8,4096]{2,1,0:T(8,128)(2,1)S(1)}, u32[]{:S(2)}, u32[]{:S(2)}) collective-permute-start(bf16[2,8,4096]{2,1,0:T(8,128)(2,1)S(1)} %pad_maximum_fusion.refs_0_), channel_id=1, source_target_pairs={{0,16},{1,17},{2,18},{3,19},{4,20},{5,21},{6,22},{7,23},{8,24},{9,... | collective-permute-start | bytes 393224 | tf_op jit(solution)/shard_map/ppermute | solution.py:39
  24.0 6.9 %collective-permute-start.3 = (bf16[2,8,4096]{2,1,0:T(8,128)(2,1)S(1)}, bf16[2,8,4096]{2,1,0:T(8,128)(2,1)S(1)}, u32[]{:S(2)}, u32[]{:S(2)}) collective-permute-start(bf16[2,8,4096]{2,1,0:T(8,128)(2,1)S(1)} %pad_maximum_fusion.refs_0_), channel_id=1, source_target_pairs={{0,24},{1,25},{2,26},{3,27},{4,28},{5,29},{6,30},{7,31},{8,0},{9,1... | collective-permute-start | bytes 393224 | tf_op jit(solution)/shard_map/ppermute | solution.py:39
  24.7 6.2 %collective-permute-start.2 = (bf16[2,8,4096]{2,1,0:T(8,128)(2,1)S(1)}, bf16[2,8,4096]{2,1,0:T(8,128)(2,1)S(1)}, u32[]{:S(2)}, u32[]{:S(2)}) collective-permute-start(bf16[2,8,4096]{2,1,0:T(8,128)(2,1)S(1)} %pad_maximum_fusion.refs_0_), channel_id=1, source_target_pairs={{0,8},{1,9},{2,10},{3,11},{4,12},{5,13},{6,14},{7,15},{8,16},{9,17... | collective-permute-start | bytes 393224 | tf_op jit(solution)/shard_map/ppermute | solution.py:39
  25.4 9.5 %copy-start.1 = (bf16[4096,512]{1,0:T(8,128)(2,1)S(1)}, bf16[4096,512]{1,0:T(8,128)(2,1)}, u32[]{:S(2)}) copy-start(bf16[4096,512]{1,0:T(8,128)(2,1)} %refs_4_.2) | copy-start | bytes 12582916
  25.5 4.6 %collective-permute-start.5 = (s32[1,8]{1,0:T(1,128)S(1)}, s32[1,8]{1,0:T(1,128)S(1)}, u32[]{:S(2)}, u32[]{:S(2)}) collective-permute-start(s32[1,8]{1,0:T(1,128)S(1)} %copy-done.4), channel_id=1, source_target_pairs={{0,192},{1,65},{2,194},{3,67},{4,196},{5,69},{6,198},{7,71},{8,200... | collective-permute-start | bytes 104 | tf_op jit(solution)/shard_map/ppermute | solution.py:39
  25.6 9.3 %collective-permute-start.13 = (bf16[2,2,8,512]{3,2,1,0:T(8,128)(2,1)S(1)}, bf16[2,2,8,512]{3,2,1,0:T(8,128)(2,1)S(1)}, u32[]{:S(2)}, u32[]{:S(2)}) collective-permute-start(bf16[2,2,8,512]{3,2,1,0:T(8,128)(2,1)S(1)} %fusion.6), channel_id=1, source_target_pairs={{0,2},{1,3},{2,0},{3,1},{4,6},{5,7},{6,4},{7,5},{8,10},{9,11},{10,... | collective-permute-start | bytes 98312 | tf_op jit(solution)/shard_map/ppermute | solution.py:39
  31.6 7.0 %copy-start = (bf16[1,8,64,4096]{3,2,1,0:T(8,128)(2,1)S(1)}, bf16[1,8,64,4096]{3,2,1,0:T(8,128)(2,1)}, u32[]{:S(2)}) copy-start(bf16[1,8,64,4096]{3,2,1,0:T(8,128)(2,1)} %param.8) | copy-start | bytes 12582916
  31.6 7.0 %copy-start.2 = (bf16[1,8,64,512]{3,2,1,0:T(8,128)(2,1)S(1)}, bf16[1,8,64,512]{3,2,1,0:T(8,128)(2,1)}, u32[]{:S(2)}) copy-start(bf16[1,8,64,512]{3,2,1,0:T(8,128)(2,1)} %param.7) | copy-start | bytes 1572868
  31.6 7.0 %copy-start.3 = (s32[1,8]{1,0:T(1,128)S(1)}, s32[1,8]{1,0:T(1,128)}, u32[]{:S(2)}) copy-start(s32[1,8]{1,0:T(1,128)} %param.10) | copy-start | bytes 100
  31.6 5.1 %collective-permute-start.8 = (bf16[2,8,8,512]{3,2,1,0:T(8,128)(2,1)S(1)}, bf16[2,8,8,512]{3,2,1,0:T(8,128)(2,1)S(1)}, u32[]{:S(2)}, u32[]{:S(2)}) collective-permute-start(bf16[2,8,8,512]{3,2,1,0:T(8,128)(2,1)S(1)} %get-tuple-element.18), channel_id=1, source_target_pairs={{0,64},{1,193},{2,66},{3,195},{4,68},{5,197},{6,70},{7,199},{8,72}... | collective-permute-start | bytes 393224 | tf_op jit(solution)/shard_map/ppermute | solution.py:39
  32.2 6.4 %collective-permute-start.9 = (bf16[2,8,8,512]{3,2,1,0:T(8,128)(2,1)S(1)}, bf16[2,8,8,512]{3,2,1,0:T(8,128)(2,1)S(1)}, u32[]{:S(2)}, u32[]{:S(2)}) collective-permute-start(bf16[2,8,8,512]{3,2,1,0:T(8,128)(2,1)S(1)} %get-tuple-element.19), channel_id=1, source_target_pairs={{0,32},{1,33},{2,34},{3,35},{4,36},{5,37},{6,38},{7,39},{8,40},{9,... | collective-permute-start | bytes 393224 | tf_op jit(solution)/shard_map/ppermute | solution.py:39
  32.2 6.4 %collective-permute-start.10 = (bf16[2,8,8,512]{3,2,1,0:T(8,128)(2,1)S(1)}, bf16[2,8,8,512]{3,2,1,0:T(8,128)(2,1)S(1)}, u32[]{:S(2)}, u32[]{:S(2)}) collective-permute-start(bf16[2,8,8,512]{3,2,1,0:T(8,128)(2,1)S(1)} %get-tuple-element.20), channel_id=1, source_target_pairs={{0,224},{1,225},{2,226},{3,227},{4,228},{5,229},{6,230},{7,231},{8... | collective-permute-start | bytes 393224 | tf_op jit(solution)/shard_map/ppermute | solution.py:39
  40.3 4.4 %collective-permute-start.14 = (bf16[32,4096]{1,0:T(8,128)(2,1)S(1)}, bf16[32,4096]{1,0:T(8,128)(2,1)S(1)}, u32[]{:S(2)}, u32[]{:S(2)}) collective-permute-start(bf16[32,4096]{1,0:T(8,128)(2,1)S(1)} %get-tuple-element.24), channel_id=1, source_target_pairs={{0,1},{1,0},{2,3},{3,2},{4,5},{5,4},{6,7},{7,6},{8,9},{9,8},{10,11... | collective-permute-start | bytes 786440 | tf_op jit(solution)/shard_map/ppermute | solution.py:39
  44.8 5.9 %collective-permute-start.15 = (bf16[8,4096]{1,0:T(8,128)(2,1)S(1)}, bf16[8,4096]{1,0:T(8,128)(2,1)S(1)}, u32[]{:S(2)}, u32[]{:S(2)}) collective-permute-start(bf16[8,4096]{1,0:T(8,128)(2,1)S(1)} %get-tuple-element.27), channel_id=1, source_target_pairs={{0,4},{1,5},{2,6},{3,7},{4,0},{5,1},{6,2},{7,3},{8,12},{9,13},{10,... | collective-permute-start | bytes 196616 | tf_op jit(solution)/shard_map/ppermute | solution.py:39
  48.5 4.3 %collective-permute-start.17 = (bf16[8,4096]{1,0:T(8,128)(2,1)S(1)}, bf16[8,4096]{1,0:T(8,128)(2,1)S(1)}, u32[]{:S(2)}, u32[]{:S(2)}) collective-permute-start(bf16[8,4096]{1,0:T(8,128)(2,1)S(1)} %get-tuple-element.28), channel_id=1, source_target_pairs={{0,6},{1,7},{2,4},{3,5},{4,2},{5,3},{6,0},{7,1},{8,14},{9,15},{10,... | collective-permute-start | bytes 196616 | tf_op jit(solution)/shard_map/ppermute | solution.py:39
  48.5 4.3 %collective-permute-start.16 = (bf16[8,4096]{1,0:T(8,128)(2,1)S(1)}, bf16[8,4096]{1,0:T(8,128)(2,1)S(1)}, u32[]{:S(2)}, u32[]{:S(2)}) collective-permute-start(bf16[8,4096]{1,0:T(8,128)(2,1)S(1)} %get-tuple-element.29), channel_id=1, source_target_pairs={{0,2},{1,3},{2,0},{3,1},{4,6},{5,7},{6,4},{7,5},{8,10},{9,11},{10,... | collective-permute-start | bytes 196616 | tf_op jit(solution)/shard_map/ppermute | solution.py:39

commit v5 on v4

--- a/solution.py
+++ b/solution.py
@@ -112,8 +112,8 @@
     )(x_t)
 
 
-def own_piece(mine, yours):
-    parts = jnp.stack([mine, other_core(yours)], 1)
+def own_piece(mine, theirs):
+    parts = jnp.stack([mine, theirs], 1)
     far = across_x(parts[2:], 2)
     near = across_x(jnp.stack([parts[1], far[1]]), 1)
     return [parts[0], near[0], far[0], near[1]]
@@ -185,9 +185,12 @@
     both = jnp.stack(
         [move(x_t, lambda z, y, x, c: ((2 * x + c + turn) % Z, y, z // 2, z % 2)) for turn in TURNS]
     )
-    own = own_piece(*halves(x_t))
-    both, asked = lax.optimization_barrier((both, far_cols))
-    asked = [asked if way == 0 else ask_z(asked, way) for way, _ in SENDS]
+    kept, given = halves(x_t)
+    theirs, early = lax.optimization_barrier((other_core(given), far_cols))
+    own = own_piece(kept, theirs)
+    soon = ask_z(early, 2)
+    both, asked, soon = lax.optimization_barrier((both, far_cols, soon))
+    asked = [soon if way == 2 else asked if way == 0 else ask_z(asked, way) for way, _ in SENDS]
     sent = pick([along_y(both, m) for m in UPS], asked)
     got = [part if way == 0 else send_z(part, way) for part, (way, _) in zip(sent, SENDS)]
     near = near_product(own, near_block)

time: 53.7 us -> 53.5 us (level)
  waiting for transfers between devices: 17 us -> 15.7 us
  starting transfers between devices: 30.9 us -> 32.1 us
    ppermute x18, waiting for transfers between devices: 17 us -> 15.7 us  [move(): return lax.ppermute(part, AXES, pairs(target))]
    ppermute x18, starting transfers between devices: 30.9 us -> 32.1 us  [move(): return lax.ppermute(part, AXES, pairs(target))]
where the time goes in v5:
time: 53.5 us; the launch traced here: 53.3 us
  starting transfers between devices  32.1 us (60%)
  waiting for transfers between devices  15.7 us (29%)
  Pallas kernels  4.6 us (9%)
  other arithmetic  0.75 us (1%)
    ppermute x18, starting transfers between devices, move(): return lax.ppermute(part, AXES, pairs(target))  32.1 us
    ppermute x18, waiting for transfers between devices, move(): return lax.ppermute(part, AXES, pairs(target))  15.7 us
    pallas_call x1, Pallas kernels, product(): pl.pallas_call(product_kernel, out_shape=(f32(32, S), bf16(32, S)), in_sp...  1.68 us
    pallas_call x1, Pallas kernels, near_product(): pl.pallas_call(near_kernel, out_shape=f32(64, S), in_specs=[VMEM] * (X +...  1.37 us
  transfers between devices with their start and end apart: 18, of which 8 were waited for; matrix products, arithmetic and copies ran while one was open for 0% of the time, Pallas kernels for 4%

profile of v5, /device:TPU:1, one launch (start us, length us, event | category | flops | bytes accessed | tf_op | source)
XLA Modules:
  0.0 53.3 jit_solution(396538648853363802)
XLA Ops:
  0.0 0.9 %halves.1 = (bf16[4,8,512]{2,1,0:T(8,128)(2,1)S(1)}, bf16[4,8,512]{2,1,0:T(8,128)(2,1)S(1)}) custom-call(bf16[8,4096]{1,0:T(8,128)(2,1)} %x_ref.1), custom_call_target="tpu_custom_call" | custom-call | flops 21474836480 | bytes 1048576 | tf_op jit(solution)/shard_map/halves/pallas_call | solution.py:104
  0.9 3.2 %collective-permute-start.2 = (bf16[4,8,512]{2,1,0:T(8,128)(2,1)S(1)}, bf16[4,8,512]{2,1,0:T(8,128)(2,1)S(1)}, u32[]{:S(2)}, u32[]{:S(2)}) collective-permute-start(bf16[4,8,512]{2,1,0:T(8,128)(2,1)S(1)} %get-tuple-element.18), channel_id=1, source_target_pairs={{0,1},{1,0},{2,3},{3,2},{4,5},{5,4},{6,7},{7,6},{8,9},{9,8},{10,11... | collective-permute-start | bytes 98312 | tf_op jit(solution)/shard_map/ppermute | solution.py:39
  4.1 1.9 %collective-permute-start = (bf16[8,4096]{1,0:T(8,128)(2,1)}, bf16[8,4096]{1,0:T(8,128)(2,1)S(1)}, u32[]{:S(2)}, u32[]{:S(2)}) collective-permute-start(bf16[8,4096]{1,0:T(8,128)(2,1)} %x_ref.1), channel_id=1, source_target_pairs={{0,0},{1,32},{2,64},{3,96},{4,128},{5,160},{6,192},{7,224},{8,8},{... | collective-permute-start | bytes 196616 | tf_op jit(solution)/shard_map/ppermute | solution.py:39
  6.0 5.5 %collective-permute-start.1 = (bf16[8,4096]{1,0:T(8,128)(2,1)}, bf16[8,4096]{1,0:T(8,128)(2,1)S(1)}, u32[]{:S(2)}, u32[]{:S(2)}) collective-permute-start(bf16[8,4096]{1,0:T(8,128)(2,1)} %x_ref.1), channel_id=1, source_target_pairs={{0,128},{1,160},{2,192},{3,224},{4,0},{5,32},{6,64},{7,96},{8,136}... | collective-permute-start | bytes 196616 | tf_op jit(solution)/shard_map/ppermute | solution.py:39
  11.6 2.4 %collective-permute-start.3 = (s32[1,8]{1,0:T(1,128)S(1)}, s32[1,8]{1,0:T(1,128)S(1)}, u32[]{:S(2)}, u32[]{:S(2)}) collective-permute-start(s32[1,8]{1,0:T(1,128)S(1)} %copy-done.4), channel_id=1, source_target_pairs={{0,192},{1,65},{2,194},{3,67},{4,196},{5,69},{6,198},{7,71},{8,200... | collective-permute-start | bytes 104 | tf_op jit(solution)/shard_map/ppermute | solution.py:39
  14.0 0.8 %collective-permute-start.12 = (bf16[2,2,8,512]{3,2,1,0:T(8,128)(2,1)S(1)}, bf16[2,2,8,512]{3,2,1,0:T(8,128)(2,1)S(1)}, u32[]{:S(2)}, u32[]{:S(2)}) collective-permute-start(bf16[2,2,8,512]{3,2,1,0:T(8,128)(2,1)S(1)} %pad_maximum_fusion.1), channel_id=1, source_target_pairs={{0,4},{1,5},{2,6},{3,7},{4,0},{5,1},{6,2},{7,3},{8,12},{9,13},{10,... | collective-permute-start | bytes 98312 | tf_op jit(solution)/shard_map/ppermute | solution.py:39
  14.7 3.4 %collective-permute-done.1 = bf16[8,4096]{1,0:T(8,128)(2,1)S(1)} collective-permute-done((bf16[8,4096]{1,0:T(8,128)(2,1)}, bf16[8,4096]{1,0:T(8,128)(2,1)S(1)}, u32[]{:S(2)}, u32[]{:S(2)}) %collective-permute-start.1) | collective-permute-done | bytes 65568 | tf_op jit(solution)/shard_map/ppermute | solution.py:39
  18.3 2.6 %collective-permute-start.7 = (s32[1,8]{1,0:T(1,128)S(1)}, s32[1,8]{1,0:T(1,128)S(1)}, u32[]{:S(2)}, u32[]{:S(2)}) collective-permute-start(s32[1,8]{1,0:T(1,128)S(1)} %copy-done.4), channel_id=1, source_target_pairs={{0,224},{1,225},{2,226},{3,227},{4,228},{5,229},{6,230},{7,231},{8... | collective-permute-start | bytes 104 | tf_op jit(solution)/shard_map/ppermute | solution.py:39
  21.0 2.9 %collective-permute-start.6 = (bf16[2,8,4096]{2,1,0:T(8,128)(2,1)S(1)}, bf16[2,8,4096]{2,1,0:T(8,128)(2,1)S(1)}, u32[]{:S(2)}, u32[]{:S(2)}) collective-permute-start(bf16[2,8,4096]{2,1,0:T(8,128)(2,1)S(1)} %pad_maximum_fusion.refs_0_), channel_id=1, source_target_pairs={{0,16},{1,17},{2,18},{3,19},{4,20},{5,21},{6,22},{7,23},{8,24},{9,... | collective-permute-start | bytes 393224 | tf_op jit(solution)/shard_map/ppermute | solution.py:39
  23.9 0.8 %collective-permute-start.5 = (bf16[2,8,4096]{2,1,0:T(8,128)(2,1)S(1)}, bf16[2,8,4096]{2,1,0:T(8,128)(2,1)S(1)}, u32[]{:S(2)}, u32[]{:S(2)}) collective-permute-start(bf16[2,8,4096]{2,1,0:T(8,128)(2,1)S(1)} %pad_maximum_fusion.refs_0_), channel_id=1, source_target_pairs={{0,24},{1,25},{2,26},{3,27},{4,28},{5,29},{6,30},{7,31},{8,0},{9,1... | collective-permute-start | bytes 393224 | tf_op jit(solution)/shard_map/ppermute | solution.py:39
  24.7 0.7 %collective-permute-start.4 = (bf16[2,8,4096]{2,1,0:T(8,128)(2,1)S(1)}, bf16[2,8,4096]{2,1,0:T(8,128)(2,1)S(1)}, u32[]{:S(2)}, u32[]{:S(2)}) collective-permute-start(bf16[2,8,4096]{2,1,0:T(8,128)(2,1)S(1)} %pad_maximum_fusion.refs_0_), channel_id=1, source_target_pairs={{0,8},{1,9},{2,10},{3,11},{4,12},{5,13},{6,14},{7,15},{8,16},{9,17... | collective-permute-start | bytes 393224 | tf_op jit(solution)/shard_map/ppermute | solution.py:39
  26.3 3.2 %collective-permute-done.5.refs_2_ = bf16[2,8,4096]{2,1,0:T(8,128)(2,1)S(1)} collective-permute-done((bf16[2,8,4096]{2,1,0:T(8,128)(2,1)S(1)}, bf16[2,8,4096]{2,1,0:T(8,128)(2,1)S(1)}, u32[]{:S(2)}, u32[]{:S(2)}) %collective-permute-start.5) | collective-permute-done | bytes 131104 | tf_op jit(solution)/shard_map/ppermute | solution.py:39
  29.8 0.7 %pick.1 = (bf16[2,8,8,512]{3,2,1,0:T(8,128)(2,1)S(1)}, bf16[2,8,8,512]{3,2,1,0:T(8,128)(2,1)S(1)}, bf16[2,8,8,512]{3,2,1,0:T(8,128)(2,1)S(1)}, bf16[2,8,8,512]{3,2,1,0:T(8,128)(2,1)S(1)}) custom-call(bf16[2,8,4096]{2,1,0:T(8,128)(2,1)S(1)} %pad_maximum_fusion.refs_0_, bf16[2,8,4096]{2,1,0:T(8,128)(2,1)S(1)} %collective-permute-done.4.refs_1_, ...), custom_call_target="tpu_custom_call" | custom-call | flops 21474836480 | bytes 1048576 | tf_op jit(solution)/shard_map/pick/pallas_call | solution.py:82
  30.5 1.7 %collective-permute-start.9 = (bf16[2,8,8,512]{3,2,1,0:T(8,128)(2,1)S(1)}, bf16[2,8,8,512]{3,2,1,0:T(8,128)(2,1)S(1)}, u32[]{:S(2)}, u32[]{:S(2)}) collective-permute-start(bf16[2,8,8,512]{3,2,1,0:T(8,128)(2,1)S(1)} %get-tuple-element.24), channel_id=1, source_target_pairs={{0,64},{1,193},{2,66},{3,195},{4,68},{5,197},{6,70},{7,199},{8,72}... | collective-permute-start | bytes 393224 | tf_op jit(solution)/shard_map/ppermute | solution.py:39
  32.2 0.8 %collective-permute-start.10 = (bf16[2,8,8,512]{3,2,1,0:T(8,128)(2,1)S(1)}, bf16[2,8,8,512]{3,2,1,0:T(8,128)(2,1)S(1)}, u32[]{:S(2)}, u32[]{:S(2)}) collective-permute-start(bf16[2,8,8,512]{3,2,1,0:T(8,128)(2,1)S(1)} %get-tuple-element.25), channel_id=1, source_target_pairs={{0,32},{1,33},{2,34},{3,35},{4,36},{5,37},{6,38},{7,39},{8,40},{9,... | collective-permute-start | bytes 393224 | tf_op jit(solution)/shard_map/ppermute | solution.py:39
  32.9 1.9 %collective-permute-start.11 = (bf16[2,8,8,512]{3,2,1,0:T(8,128)(2,1)S(1)}, bf16[2,8,8,512]{3,2,1,0:T(8,128)(2,1)S(1)}, u32[]{:S(2)}, u32[]{:S(2)}) collective-permute-start(bf16[2,8,8,512]{3,2,1,0:T(8,128)(2,1)S(1)} %get-tuple-element.26), channel_id=1, source_target_pairs={{0,224},{1,225},{2,226},{3,227},{4,228},{5,229},{6,230},{7,231},{8... | collective-permute-start | bytes 393224 | tf_op jit(solution)/shard_map/ppermute | solution.py:39
  34.9 1.4 %near.1.refs_5_ = f32[64,4096]{1,0:T(8,128)S(1)} custom-call(bf16[2,8,512]{2,1,0:T(8,128)(2,1)S(1)} %maximum_bitcast_fusion.refs_0_, bf16[2,8,512]{2,1,0:T(8,128)(2,1)S(1)} %get-tuple-element.37.refs_1_, bf16[2,8,512]{2,1,0:T(8,128)(2,1)S(1)} %get-tuple-element.38.refs_2_, bf16[2,8,512]{2,1,0:T(8,128)(2,1)S(1)} %get-tuple-element.36.refs_3_, ...), custom_call_target="tpu_custom_call" | custom-call | flops 268435456 | bytes 5242880 | tf_op jit(solution)/shard_map/near/pallas_call | solution.py:132
  36.2 3.7 %collective-permute-done.10.refs_2_ = bf16[2,8,8,512]{3,2,1,0:T(8,128)(2,1)S(1)} collective-permute-done((bf16[2,8,8,512]{3,2,1,0:T(8,128)(2,1)S(1)}, bf16[2,8,8,512]{3,2,1,0:T(8,128)(2,1)S(1)}, u32[]{:S(2)}, u32[]{:S(2)}) %collective-permute-start.10) | collective-permute-done | bytes 131104 | tf_op jit(solution)/shard_map/ppermute | solution.py:39
  39.9 1.7 %product.1 = (f32[32,4096]{1,0:T(8,128)S(1)}, bf16[32,4096]{1,0:T(8,128)(2,1)S(1)}) custom-call(s32[8]{0:T(128)S(1)} %bitcast.20, bf16[2,8,8,512]{3,2,1,0:T(8,128)(2,1)S(1)} %get-tuple-element.23.refs_0_, bf16[2,8,8,512]{3,2,1,0:T(8,128)(2,1)S(1)} %collective-permute-done.9.refs_1_, bf16[2,8,8,512]{3,2,1,0:T(8,128)(2,1)S(1)} %collective-permute-done.10.refs_2_, ...), custom_call_target="tpu_custom_call" | custom-call | flops 536870912 | bytes 10485760 | tf_op jit(solution)/shard_map/product/pallas_call | solution.py:172
  41.6 2.3 %collective-permute-start.14 = (bf16[32,4096]{1,0:T(8,128)(2,1)S(1)}, bf16[32,4096]{1,0:T(8,128)(2,1)S(1)}, u32[]{:S(2)}, u32[]{:S(2)}) collective-permute-start(bf16[32,4096]{1,0:T(8,128)(2,1)S(1)} %get-tuple-element.30), channel_id=1, source_target_pairs={{0,1},{1,0},{2,3},{3,2},{4,5},{5,4},{6,7},{7,6},{8,9},{9,8},{10,11... | collective-permute-start | bytes 786440 | tf_op jit(solution)/shard_map/ppermute | solution.py:39
  43.9 1.2 %collective-permute-done.14 = bf16[32,4096]{1,0:T(8,128)(2,1)S(1)} collective-permute-done((bf16[32,4096]{1,0:T(8,128)(2,1)S(1)}, bf16[32,4096]{1,0:T(8,128)(2,1)S(1)}, u32[]{:S(2)}, u32[]{:S(2)}) %collective-permute-start.14) | collective-permute-done | bytes 262176 | tf_op jit(solution)/shard_map/ppermute | solution.py:39
  45.1 3.2 %collective-permute-start.15 = (bf16[8,4096]{1,0:T(8,128)(2,1)S(1)}, bf16[8,4096]{1,0:T(8,128)(2,1)S(1)}, u32[]{:S(2)}, u32[]{:S(2)}) collective-permute-start(bf16[8,4096]{1,0:T(8,128)(2,1)S(1)} %get-tuple-element.33), channel_id=1, source_target_pairs={{0,4},{1,5},{2,6},{3,7},{4,0},{5,1},{6,2},{7,3},{8,12},{9,13},{10,... | collective-permute-start | bytes 196616 | tf_op jit(solution)/shard_map/ppermute | solution.py:39
  49.2 0.8 %collective-permute-done.15 = bf16[8,4096]{1,0:T(8,128)(2,1)S(1)} collective-permute-done((bf16[8,4096]{1,0:T(8,128)(2,1)S(1)}, bf16[8,4096]{1,0:T(8,128)(2,1)S(1)}, u32[]{:S(2)}, u32[]{:S(2)}) %collective-permute-start.15) | collective-permute-done | bytes 65568 | tf_op jit(solution)/shard_map/ppermute | solution.py:39
  50.0 2.7 %collective-permute-done.17 = bf16[8,4096]{1,0:T(8,128)(2,1)S(1)} collective-permute-done((bf16[8,4096]{1,0:T(8,128)(2,1)S(1)}, bf16[8,4096]{1,0:T(8,128)(2,1)S(1)}, u32[]{:S(2)}, u32[]{:S(2)}) %collective-permute-start.17) | collective-permute-done | bytes 65568 | tf_op jit(solution)/shard_map/ppermute | solution.py:39
  (35 shorter events, 3.0 us)
Async XLA Ops:
  0.0 11.6 %copy-start.4 = (s32[1,8]{1,0:T(1,128)S(1)}, s32[1,8]{1,0:T(1,128)}, u32[]{:S(2)}) copy-start(s32[1,8]{1,0:T(1,128)} %refs_4_.1) | copy-start | bytes 100
  0.9 10.7 %collective-permute-start.2 = (bf16[4,8,512]{2,1,0:T(8,128)(2,1)S(1)}, bf16[4,8,512]{2,1,0:T(8,128)(2,1)S(1)}, u32[]{:S(2)}, u32[]{:S(2)}) collective-permute-start(bf16[4,8,512]{2,1,0:T(8,128)(2,1)S(1)} %get-tuple-element.18), channel_id=1, source_target_pairs={{0,1},{1,0},{2,3},{3,2},{4,5},{5,4},{6,7},{7,6},{8,9},{9,8},{10,11... | collective-permute-start | bytes 98312 | tf_op jit(solution)/shard_map/ppermute | solution.py:39
  4.1 10.6 %collective-permute-start = (bf16[8,4096]{1,0:T(8,128)(2,1)}, bf16[8,4096]{1,0:T(8,128)(2,1)S(1)}, u32[]{:S(2)}, u32[]{:S(2)}) collective-permute-start(bf16[8,4096]{1,0:T(8,128)(2,1)} %x_ref.1), channel_id=1, source_target_pairs={{0,0},{1,32},{2,64},{3,96},{4,128},{5,160},{6,192},{7,224},{8,8},{... | collective-permute-start | bytes 196616 | tf_op jit(solution)/shard_map/ppermute | solution.py:39
  6.0 12.2 %collective-permute-start.1 = (bf16[8,4096]{1,0:T(8,128)(2,1)}, bf16[8,4096]{1,0:T(8,128)(2,1)S(1)}, u32[]{:S(2)}, u32[]{:S(2)}) collective-permute-start(bf16[8,4096]{1,0:T(8,128)(2,1)} %x_ref.1), channel_id=1, source_target_pairs={{0,128},{1,160},{2,192},{3,224},{4,0},{5,32},{6,64},{7,96},{8,136}... | collective-permute-start | bytes 196616 | tf_op jit(solution)/shard_map/ppermute | solution.py:39
  11.6 6.6 %collective-permute-start.3 = (s32[1,8]{1,0:T(1,128)S(1)}, s32[1,8]{1,0:T(1,128)S(1)}, u32[]{:S(2)}, u32[]{:S(2)}) collective-permute-start(s32[1,8]{1,0:T(1,128)S(1)} %copy-done.4), channel_id=1, source_target_pairs={{0,192},{1,65},{2,194},{3,67},{4,196},{5,69},{6,198},{7,71},{8,200... | collective-permute-start | bytes 104 | tf_op jit(solution)/shard_map/ppermute | solution.py:39
  14.0 10.7 %collective-permute-start.12 = (bf16[2,2,8,512]{3,2,1,0:T(8,128)(2,1)S(1)}, bf16[2,2,8,512]{3,2,1,0:T(8,128)(2,1)S(1)}, u32[]{:S(2)}, u32[]{:S(2)}) collective-permute-start(bf16[2,2,8,512]{3,2,1,0:T(8,128)(2,1)S(1)} %pad_maximum_fusion.1), channel_id=1, source_target_pairs={{0,4},{1,5},{2,6},{3,7},{4,0},{5,1},{6,2},{7,3},{8,12},{9,13},{10,... | collective-permute-start | bytes 98312 | tf_op jit(solution)/shard_map/ppermute | solution.py:39
  18.2 7.2 %collective-permute-start.8 = (s32[1,8]{1,0:T(1,128)S(1)}, s32[1,8]{1,0:T(1,128)S(1)}, u32[]{:S(2)}, u32[]{:S(2)}) collective-permute-start(s32[1,8]{1,0:T(1,128)S(1)} %copy-done.4), channel_id=1, source_target_pairs={{0,32},{1,33},{2,34},{3,35},{4,36},{5,37},{6,38},{7,39},{8,40},{9,... | collective-permute-start | bytes 104 | tf_op jit(solution)/shard_map/ppermute | solution.py:39
  18.3 7.5 %collective-permute-start.7 = (s32[1,8]{1,0:T(1,128)S(1)}, s32[1,8]{1,0:T(1,128)S(1)}, u32[]{:S(2)}, u32[]{:S(2)}) collective-permute-start(s32[1,8]{1,0:T(1,128)S(1)} %copy-done.4), channel_id=1, source_target_pairs={{0,224},{1,225},{2,226},{3,227},{4,228},{5,229},{6,230},{7,231},{8... | collective-permute-start | bytes 104 | tf_op jit(solution)/shard_map/ppermute | solution.py:39
  21.0 5.3 %collective-permute-start.6 = (bf16[2,8,4096]{2,1,0:T(8,128)(2,1)S(1)}, bf16[2,8,4096]{2,1,0:T(8,128)(2,1)S(1)}, u32[]{:S(2)}, u32[]{:S(2)}) collective-permute-start(bf16[2,8,4096]{2,1,0:T(8,128)(2,1)S(1)} %pad_maximum_fusion.refs_0_), channel_id=1, source_target_pairs={{0,16},{1,17},{2,18},{3,19},{4,20},{5,21},{6,22},{7,23},{8,24},{9,... | collective-permute-start | bytes 393224 | tf_op jit(solution)/shard_map/ppermute | solution.py:39
  23.9 5.6 %collective-permute-start.5 = (bf16[2,8,4096]{2,1,0:T(8,128)(2,1)S(1)}, bf16[2,8,4096]{2,1,0:T(8,128)(2,1)S(1)}, u32[]{:S(2)}, u32[]{:S(2)}) collective-permute-start(bf16[2,8,4096]{2,1,0:T(8,128)(2,1)S(1)} %pad_maximum_fusion.refs_0_), channel_id=1, source_target_pairs={{0,24},{1,25},{2,26},{3,27},{4,28},{5,29},{6,30},{7,31},{8,0},{9,1... | collective-permute-start | bytes 393224 | tf_op jit(solution)/shard_map/ppermute | solution.py:39
  24.7 5.1 %collective-permute-start.4 = (bf16[2,8,4096]{2,1,0:T(8,128)(2,1)S(1)}, bf16[2,8,4096]{2,1,0:T(8,128)(2,1)S(1)}, u32[]{:S(2)}, u32[]{:S(2)}) collective-permute-start(bf16[2,8,4096]{2,1,0:T(8,128)(2,1)S(1)} %pad_maximum_fusion.refs_0_), channel_id=1, source_target_pairs={{0,8},{1,9},{2,10},{3,11},{4,12},{5,13},{6,14},{7,15},{8,16},{9,17... | collective-permute-start | bytes 393224 | tf_op jit(solution)/shard_map/ppermute | solution.py:39
  25.4 9.5 %copy-start.1 = (bf16[4096,512]{1,0:T(8,128)(2,1)S(1)}, bf16[4096,512]{1,0:T(8,128)(2,1)}, u32[]{:S(2)}) copy-start(bf16[4096,512]{1,0:T(8,128)(2,1)} %refs_4_.2) | copy-start | bytes 12582916
  25.4 9.5 %collective-permute-start.13 = (bf16[2,2,8,512]{3,2,1,0:T(8,128)(2,1)S(1)}, bf16[2,2,8,512]{3,2,1,0:T(8,128)(2,1)S(1)}, u32[]{:S(2)}, u32[]{:S(2)}) collective-permute-start(bf16[2,2,8,512]{3,2,1,0:T(8,128)(2,1)S(1)} %fusion.6), channel_id=1, source_target_pairs={{0,2},{1,3},{2,0},{3,1},{4,6},{5,7},{6,4},{7,5},{8,10},{9,11},{10,... | collective-permute-start | bytes 98312 | tf_op jit(solution)/shard_map/ppermute | solution.py:39
  30.4 9.5 %copy-start = (bf16[1,8,64,4096]{3,2,1,0:T(8,128)(2,1)S(1)}, bf16[1,8,64,4096]{3,2,1,0:T(8,128)(2,1)}, u32[]{:S(2)}) copy-start(bf16[1,8,64,4096]{3,2,1,0:T(8,128)(2,1)} %param.8) | copy-start | bytes 12582916
  30.5 9.5 %copy-start.2 = (bf16[1,8,64,512]{3,2,1,0:T(8,128)(2,1)S(1)}, bf16[1,8,64,512]{3,2,1,0:T(8,128)(2,1)}, u32[]{:S(2)}) copy-start(bf16[1,8,64,512]{3,2,1,0:T(8,128)(2,1)} %param.7) | copy-start | bytes 1572868
  30.5 9.5 %copy-start.3 = (s32[1,8]{1,0:T(1,128)S(1)}, s32[1,8]{1,0:T(1,128)}, u32[]{:S(2)}) copy-start(s32[1,8]{1,0:T(1,128)} %param.10) | copy-start | bytes 100
  30.5 5.8 %collective-permute-start.9 = (bf16[2,8,8,512]{3,2,1,0:T(8,128)(2,1)S(1)}, bf16[2,8,8,512]{3,2,1,0:T(8,128)(2,1)S(1)}, u32[]{:S(2)}, u32[]{:S(2)}) collective-permute-start(bf16[2,8,8,512]{3,2,1,0:T(8,128)(2,1)S(1)} %get-tuple-element.24), channel_id=1, source_target_pairs={{0,64},{1,193},{2,66},{3,195},{4,68},{5,197},{6,70},{7,199},{8,72}... | collective-permute-start | bytes 393224 | tf_op jit(solution)/shard_map/ppermute | solution.py:39
  32.2 7.7 %collective-permute-start.10 = (bf16[2,8,8,512]{3,2,1,0:T(8,128)(2,1)S(1)}, bf16[2,8,8,512]{3,2,1,0:T(8,128)(2,1)S(1)}, u32[]{:S(2)}, u32[]{:S(2)}) collective-permute-start(bf16[2,8,8,512]{3,2,1,0:T(8,128)(2,1)S(1)} %get-tuple-element.25), channel_id=1, source_target_pairs={{0,32},{1,33},{2,34},{3,35},{4,36},{5,37},{6,38},{7,39},{8,40},{9,... | collective-permute-start | bytes 393224 | tf_op jit(solution)/shard_map/ppermute | solution.py:39
  32.9 7.0 %collective-permute-start.11 = (bf16[2,8,8,512]{3,2,1,0:T(8,128)(2,1)S(1)}, bf16[2,8,8,512]{3,2,1,0:T(8,128)(2,1)S(1)}, u32[]{:S(2)}, u32[]{:S(2)}) collective-permute-start(bf16[2,8,8,512]{3,2,1,0:T(8,128)(2,1)S(1)} %get-tuple-element.26), channel_id=1, source_target_pairs={{0,224},{1,225},{2,226},{3,227},{4,228},{5,229},{6,230},{7,231},{8... | collective-permute-start | bytes 393224 | tf_op jit(solution)/shard_map/ppermute | solution.py:39
  41.6 3.4 %collective-permute-start.14 = (bf16[32,4096]{1,0:T(8,128)(2,1)S(1)}, bf16[32,4096]{1,0:T(8,128)(2,1)S(1)}, u32[]{:S(2)}, u32[]{:S(2)}) collective-permute-start(bf16[32,4096]{1,0:T(8,128)(2,1)S(1)} %get-tuple-element.30), channel_id=1, source_target_pairs={{0,1},{1,0},{2,3},{3,2},{4,5},{5,4},{6,7},{7,6},{8,9},{9,8},{10,11... | collective-permute-start | bytes 786440 | tf_op jit(solution)/shard_map/ppermute | solution.py:39
  45.1 4.8 %collective-permute-start.15 = (bf16[8,4096]{1,0:T(8,128)(2,1)S(1)}, bf16[8,4096]{1,0:T(8,128)(2,1)S(1)}, u32[]{:S(2)}, u32[]{:S(2)}) collective-permute-start(bf16[8,4096]{1,0:T(8,128)(2,1)S(1)} %get-tuple-element.33), channel_id=1, source_target_pairs={{0,4},{1,5},{2,6},{3,7},{4,0},{5,1},{6,2},{7,3},{8,12},{9,13},{10,... | collective-permute-start | bytes 196616 | tf_op jit(solution)/shard_map/ppermute | solution.py:39
  48.3 4.3 %collective-permute-start.17 = (bf16[8,4096]{1,0:T(8,128)(2,1)S(1)}, bf16[8,4096]{1,0:T(8,128)(2,1)S(1)}, u32[]{:S(2)}, u32[]{:S(2)}) collective-permute-start(bf16[8,4096]{1,0:T(8,128)(2,1)S(1)} %get-tuple-element.34), channel_id=1, source_target_pairs={{0,6},{1,7},{2,4},{3,5},{4,2},{5,3},{6,0},{7,1},{8,14},{9,15},{10,... | collective-permute-start | bytes 196616 | tf_op jit(solution)/shard_map/ppermute | solution.py:39
  48.9 3.7 %collective-permute-start.16 = (bf16[8,4096]{1,0:T(8,128)(2,1)S(1)}, bf16[8,4096]{1,0:T(8,128)(2,1)S(1)}, u32[]{:S(2)}, u32[]{:S(2)}) collective-permute-start(bf16[8,4096]{1,0:T(8,128)(2,1)S(1)} %get-tuple-element.35), channel_id=1, source_target_pairs={{0,2},{1,3},{2,0},{3,1},{4,6},{5,7},{6,4},{7,5},{8,10},{9,11},{10,... | collective-permute-start | bytes 196616 | tf_op jit(solution)/shard_map/ppermute | solution.py:39
